TPU v7x, 256 devices: a whole 4x4x8 slice. The times are simulated.
256 devices in a mesh: ctx: 32 (over z, y), head: 8 (over x, core).
Axes of the slice: x: 4, y: 4, z: 8, core: 2. Of those that a mesh axis runs over, the one named last changes fastest.
Arguments:
- queries: bfloat16 [8192, 8192], P('ctx', 'head'), may hold values from -6 to 6
- key_rows: bfloat16 [8192, 1024], P('ctx', 'head'), may hold values from -6 to 6
- value_rows: bfloat16 [8192, 1024], P('ctx', 'head'), may hold values from -6 to 6
- out_grads: bfloat16 [8192, 8192], P(('ctx', 'head')), may hold values from -6 to 6
- doc_ids: int32 [8192], replicated, may hold values from 0 to 7, never falling along the last dimension, each value on 1 to 4096 neighbouring positions
- owner_plan: int32 [32, 32], replicated, may hold values from 0 to 31, each once within a row
Outputs:
- attention: bfloat16 [8192, 8192], P(('ctx', 'head'))
- query_grads: bfloat16 [8192, 8192], P('ctx', 'head')
- key_grads: bfloat16 [8192, 1024], P('ctx', 'head')
- value_grads: bfloat16 [8192, 1024], P('ctx', 'head')
Inputs may be any that keep to these rules, and one draw needn't show every extreme that they name: `owner_plan`: row d lists the owners of the 32 pieces of index d of ctx; each owner once in every row.
All inputs are finite; a program needn't handle non-finite values.
Results may differ from a plain program's by a relative error of at most 0.027.
Values may be sent and summed in bfloat16 or wider, within the bound.
No kernel may reach another device: no remote copies, remote signals or barrier semaphores. Data moves between devices by JAX's collectives and lax.ppermute only.
A program may use at most 64 MiB of HBM per device.

v0:
```python
import jax
import jax.numpy as jnp
from jax import lax
from jax.experimental import pallas as pl
from jax.experimental.pallas import tpu as pltpu
from jax.sharding import PartitionSpec as P

HD = 128
NZ = 8
NY = 4
TOK = 256
PIECE = 8
KB = 512
DOCLEN = 4096
DOCS = 8
GROUPS = 8
MASKED = -1e30
LOG2E = 1.4426950408889634
f32 = jnp.float32
bf16 = jnp.bfloat16


def attend_kernel(
    lo_ref, hi_ref, at_ref, place_ref, start_ref, q_ref, g_ref, *refs
):
    k_refs, v_refs = refs[:NZ], refs[NZ : NZ + 5]
    o_ref, dq_ref = refs[NZ + 5 : NZ + 7]
    dk_refs = refs[NZ + 7 : 2 * NZ + 7]
    dv_refs = refs[2 * NZ + 7 : 2 * NZ + 15]
    kt, vt, kn, vn, dk_acc, dv_acc, s_ref, e_ref = refs[2 * NZ + 15 :]
    rows, width = q_ref.shape
    heads = width // HD
    span = rows // GROUPS
    lanes = span * heads
    scale = HD**-0.5
    zc = NY * TOK
    my_z, my_y = at_ref[0], at_ref[1]

    for s in range(NZ):
        z = lax.rem(my_z + NZ - s, NZ)
        at = pl.ds(pl.multiple_of(z * zc, zc), zc)
        kn[at, :] = k_refs[s][...]
        for b in range(zc // KB):
            kt[z * (zc // KB) + b] = k_refs[s][b * KB : (b + 1) * KB, :].T

    def place_v(ref, shift, z_from, z_count):
        y = lax.rem(my_y + NY - shift, NY)
        for z in range(z_count):
            at = pl.ds(pl.multiple_of((z_from + z) * zc + y * TOK, TOK), TOK)
            vn[at, :] = ref[z * TOK : (z + 1) * TOK, :]

    place_v(v_refs[0], 0, 0, NZ)
    place_v(v_refs[1], 1, 0, NZ)
    place_v(v_refs[2], 3, 0, NZ)
    place_v(v_refs[3], 2, 0, NZ // 2)
    place_v(v_refs[4], 2, NZ // 2, NZ // 2)

    def prepare(b, carry):
        at = pl.ds(pl.multiple_of(b * KB, KB), KB)
        vt[b] = vn[at, :].T
        dk_acc[at, :] = jnp.zeros((KB, HD), f32)
        dv_acc[at, :] = jnp.zeros((KB, HD), f32)
        return carry

    lax.fori_loop(0, NZ * zc // KB, prepare, 0)

    def gather_heads(ref, at):
        x = ref[at, :]
        return jnp.concatenate([x[:, h * HD : (h + 1) * HD] for h in range(heads)], axis=0)

    def scatter_heads(ref, at, x):
        for h in range(heads):
            ref[at, h * HD : (h + 1) * HD] = x[h * span : (h + 1) * span]

    def group(gi, carry):
        at = pl.ds(pl.multiple_of(gi * span, span), span)
        lo, hi = lo_ref[gi], hi_ref[gi]
        place, start = place_ref[gi], start_ref[gi]
        qt = gather_heads(q_ref, at).astype(f32).T
        gt = gather_heads(g_ref, at).astype(f32).T
        qtb, gtb = qt.astype(bf16), gt.astype(bf16)

        def score(kb, peak):
            keys = pl.ds(pl.multiple_of(kb * KB, KB), KB)
            s = jnp.dot(kn[keys, :], qtb, preferred_element_type=f32)
            u = kb * KB + lax.broadcasted_iota(jnp.int32, (KB, lanes), 0)
            s = jnp.where((u >= start) & (u <= place), s, MASKED)
            s_ref[kb - lo] = s
            return jnp.maximum(peak, jnp.max(s.reshape(KB // 8, 8, lanes), axis=0))

        peak = lax.fori_loop(lo, hi, score, jnp.full((8, lanes), MASKED, f32))
        peak = jnp.max(peak, axis=0, keepdims=True) * (scale * LOG2E)

        def weigh(kb, carry):
            ot, total = carry
            e = jnp.exp2(s_ref[kb - lo] * (scale * LOG2E) - peak)
            eb = e.astype(bf16)
            e_ref[kb - lo] = eb
            total = total + jnp.sum(e.reshape(KB // 8, 8, lanes), axis=0)
            ot = ot + jnp.dot(vt[kb], eb, preferred_element_type=f32)
            return ot, total

        ot, total = lax.fori_loop(
            lo, hi, weigh, (jnp.zeros((HD, lanes), f32), jnp.zeros((8, lanes), f32))
        )
        inverse = 1.0 / jnp.sum(total, axis=0, keepdims=True)
        otb = (ot * inverse).astype(bf16).astype(f32)
        scatter_heads(o_ref, at, otb.T.astype(bf16))
        delta = jnp.sum(otb * gt, axis=0, keepdims=True)
        qs = (qt * inverse).T.astype(bf16)
        gs = (gt * inverse).T.astype(bf16)

        def back(kb, dqt):
            keys = pl.ds(pl.multiple_of(kb * KB, KB), KB)
            dp = jnp.dot(vn[keys, :], gtb, preferred_element_type=f32)
            eb = e_ref[kb - lo]
            ds = (eb.astype(f32) * (dp - delta)).astype(bf16)
            dk_acc[keys, :] += jnp.dot(ds, qs, preferred_element_type=f32)
            dv_acc[keys, :] += jnp.dot(eb, gs, preferred_element_type=f32)
            return dqt + jnp.dot(kt[kb], ds, preferred_element_type=f32)

        dqt = lax.fori_loop(lo, hi, back, jnp.zeros((HD, lanes), f32))
        scatter_heads(dq_ref, at, (dqt * (inverse * scale)).T.astype(bf16))
        return carry

    lax.fori_loop(0, GROUPS, group, 0)

    for r in range(NZ):
        z = lax.rem(my_z + r, NZ)
        at = pl.ds(pl.multiple_of(z * zc, zc), zc)
        dk_refs[r][...] = (dk_acc[at, :] * scale).astype(bf16)
    for r in range(NY):
        y = lax.rem(my_y + r, NY)
        for z in range(NZ):
            half, inside = divmod(z, NZ // 2)
            at = pl.ds(pl.multiple_of(z * zc + y * TOK, TOK), TOK)
            dv_refs[2 * r + half][inside * TOK : (inside + 1) * TOK, :] = dv_acc[at, :].astype(bf16)


def attend(lo, hi, at, place, start, q, g, ks, vs):
    rows, width = q.shape
    total = NZ * NY * TOK
    lanes = rows // GROUPS * (width // HD)
    most = (DOCLEN + rows // GROUPS // PIECE * TOK) // KB
    vm = pl.BlockSpec(memory_space=pltpu.VMEM)
    sm = pl.BlockSpec(memory_space=pltpu.SMEM)
    outs = (
        [jax.ShapeDtypeStruct((rows, width), bf16)] * 2
        + [jax.ShapeDtypeStruct((NY * TOK, HD), bf16)] * NZ
        + [jax.ShapeDtypeStruct((NZ // 2 * TOK, HD), bf16)] * (2 * NY)
    )
    out = pl.pallas_call(
        attend_kernel,
        in_specs=[sm] * 3 + [vm] * (4 + len(ks) + len(vs)),
        out_specs=[vm] * len(outs),
        out_shape=outs,
        scratch_shapes=[
            pltpu.VMEM((total // KB, HD, KB), bf16),
            pltpu.VMEM((total // KB, HD, KB), bf16),
            pltpu.VMEM((total, HD), bf16),
            pltpu.VMEM((total, HD), bf16),
            pltpu.VMEM((total, HD), f32),
            pltpu.VMEM((total, HD), f32),
            pltpu.VMEM((most, KB, lanes), f32),
            pltpu.VMEM((most, KB, lanes), bf16),
        ],
        compiler_params=pltpu.CompilerParams(vmem_limit_bytes=56 * 1024 * 1024),
        cost_estimate=pl.CostEstimate(
            flops=12 * 10**9, bytes_accessed=12 * 10**6, transcendentals=4 * 10**6
        ),
        name="attend",
    )(lo, hi, at, place, start, q, g, *ks, *vs)
    return out[0], out[1], out[2 : 2 + NZ], out[2 + NZ :]


def shift(x, dz, dy):
    pairs = [
        (z * NY + y, (z + dz) % NZ * NY + (y + dy) % NY) for z in range(NZ) for y in range(NY)
    ]
    return lax.ppermute(x, "ctx", pairs)


Z_GROUPS = [[z * NY + y for z in range(NZ)] for y in range(NY)]
Y_GROUPS = [[z * NY + y for y in range(NY)] for z in range(NZ)]


def swap(x, groups):
    return lax.all_to_all(x, "ctx", 0, 0, axis_index_groups=groups, tiled=True)


def spread(x, groups):
    n = len(groups[0])
    return swap(jnp.broadcast_to(x[None], (n,) + x.shape), groups).reshape(n * x.shape[0], x.shape[1])


def add(a, *more):
    total = a.astype(f32)
    for x in more:
        total = total + x.astype(f32)
    return total.astype(bf16)


def body(queries, key_rows, value_rows, out_grads, doc_ids, owner_plan):
    n = NZ * NY
    me = lax.axis_index("ctx")
    rows, width = queries.shape
    pieces = jnp.arange(n, dtype=jnp.int32)
    my_owners = lax.dynamic_index_in_dim(owner_plan, me, 0, keepdims=False)

    r = jnp.arange(rows, dtype=jnp.int32)
    owner_row = jnp.repeat(my_owners, PIECE) * PIECE + r % PIECE
    onehot = (r[:, None] == owner_row[None, :]).astype(bf16)

    outgoing = jnp.dot(onehot, queries, preferred_element_type=f32).astype(bf16)
    q = lax.all_to_all(outgoing.reshape(n, PIECE, width), "ctx", 0, 0, tiled=True).reshape(rows, width)
    g = lax.all_to_all(out_grads, "head", split_axis=1, concat_axis=0, tiled=True)

    k_own = spread(key_rows, Y_GROUPS)
    ups, downs = [k_own], [k_own]
    for step in range(NZ // 2):
        ups.append(shift(ups[-1], 1, 0))
        if step < NZ // 2 - 1:
            downs.append(shift(downs[-1], -1, 0))
    ks = ups + downs[:0:-1]

    v_own = spread(value_rows, Z_GROUPS)
    v_up, v_down = shift(v_own, 0, 1), shift(v_own, 0, -1)
    half = v_own.shape[0] // 2
    vs = [v_own, v_up, v_down, shift(v_up[:half], 0, 1), shift(v_down[half:], 0, -1)]

    slot_of = jnp.sum(jnp.where(owner_plan == me, pieces[None, :], 0), axis=1)
    place = (
        pieces[:, None] * TOK + slot_of[:, None] * PIECE + jnp.arange(PIECE, dtype=jnp.int32)[None, :]
    ).reshape(GROUPS, 1, 1, rows // GROUPS)
    docs = jnp.arange(DOCS, dtype=jnp.int32)
    doc_first = jnp.sum((doc_ids[:, None] < docs[None, :]).astype(jnp.int32), axis=0)
    start = jnp.max(jnp.where(doc_first <= place[..., None], doc_first, 0), axis=-1)
    lo = jnp.min(start, axis=(1, 2, 3)) // KB
    hi = jnp.max(place, axis=(1, 2, 3)) // KB + 1
    spread_lanes = lambda x: jnp.broadcast_to(x, (GROUPS, 1, width // HD, rows // GROUPS)).reshape(GROUPS, 1, -1)
    at = jnp.stack([me // NY, me % NY])

    o, dq, dks, dvs = attend(lo, hi, at, spread_lanes(place), spread_lanes(start), q, g, ks, vs)

    returned = lax.all_to_all(dq.reshape(n, PIECE, width), "ctx", 0, 0, tiled=True).reshape(rows, width)
    attention = lax.all_to_all(o, "head", split_axis=0, concat_axis=1, tiled=True)

    up, down = dks[4], dks[5]
    up = add(dks[3], shift(up, 1, 0))
    for i in (2, 1):
        up = add(dks[i], shift(up, 1, 0))
        down = add(dks[8 - i], shift(down, -1, 0))
    k_sum = add(dks[0], shift(up, 1, 0), shift(down, -1, 0))
    key_grads = jnp.sum(swap(k_sum.reshape(NY, TOK, HD), Y_GROUPS).astype(f32), axis=0).astype(bf16)

    a_up = add(dvs[2], shift(dvs[4], 0, 1))
    b_down = add(dvs[7], shift(dvs[5], 0, -1))
    a_sum = add(dvs[0], shift(dvs[6], 0, -1), shift(a_up, 0, 1))
    b_sum = add(dvs[1], shift(dvs[3], 0, 1), shift(b_down, 0, -1))
    v_sum = jnp.concatenate([a_sum, b_sum], axis=0).reshape(NZ, TOK, HD)
    value_grads = jnp.sum(swap(v_sum, Z_GROUPS).astype(f32), axis=0).astype(bf16)

    query_grads = jnp.dot(onehot.T, returned, preferred_element_type=f32).astype(bf16)
    return attention, query_grads, key_grads, value_grads


def solution(mesh):
    return jax.shard_map(
        body,
        mesh=mesh,
        in_specs=(P("ctx", "head"),) * 3 + (P(("ctx", "head"), None), P(), P()),
        out_specs=(P(("ctx", "head"), None),) + (P("ctx", "head"),) * 3,
        check_vma=False,
    )
```

profile of v0, /device:TPU:2, one launch (start us, length us, event | category | flops | bytes accessed | tf_op | source)
XLA Modules:
  0.0 219.7 jit_solution(11479726004374387591)
XLA Ops:
  2.3 4.5 %all-to-all-start.2 = ((bf16[4,256,128]{2,1,0:T(8,128)(2,1)}), bf16[4,256,128]{2,1,0:T(8,128)(2,1)S(1)}, u32[]{:S(2)}, u32[]{:S(2)}) async-start(bf16[4,256,128]{2,1,0:T(8,128)(2,1)} %broadcast_in_dim.64), calls=%async_computation.2 | async-start | bytes 524288 | tf_op jit(solution)/shard_map/all_to_all | solution.py:188
  6.8 6.6 %all-to-all-done.2 = bf16[4,256,128]{2,1,0:T(8,128)(2,1)S(1)} async-done(((bf16[4,256,128]{2,1,0:T(8,128)(2,1)}), bf16[4,256,128]{2,1,0:T(8,128)(2,1)S(1)}, u32[]{:S(2)}, u32[]{:S(2)}) %all-to-all-start.2) | async-done | bytes 262176 | tf_op jit(solution)/shard_map/all_to_all | solution.py:188
  13.5 13.8 %all_to_all.68 = bf16[32,8,1024]{2,0,1:T(8,128)(2,1)} all-to-all(bf16[32,8,1024]{2,0,1:T(8,128)(2,1)S(1)} %bitcast.30), channel_id=1, replica_groups=mesh['ctx'=32,'head'=8] {'head'}, dimensions={1} | all-to-all | bytes 1048576 | tf_op jit(solution)/shard_map/all_to_all | solution.py:216
  28.1 8.6 %all-to-all-start.3 = ((bf16[8,256,128]{2,1,0:T(8,128)(2,1)}), bf16[8,256,128]{2,1,0:T(8,128)(2,1)S(1)}, u32[]{:S(2)}, u32[]{:S(2)}) async-start(bf16[8,256,128]{2,1,0:T(8,128)(2,1)} %broadcast_in_dim.65), calls=%async_computation.3 | async-start | bytes 1048576 | tf_op jit(solution)/shard_map/all_to_all | solution.py:188
  41.6 15.2 %collective-permute-done.refs_1_ = bf16[1024,128]{1,0:T(8,128)(2,1)S(1)} collective-permute-done((bf16[1024,128]{1,0:T(8,128)(2,1)S(1)}, bf16[1024,128]{1,0:T(8,128)(2,1)S(1)}, u32[]{:S(2)}, u32[]{:S(2)}) %collective-permute-start) | collective-permute-done | bytes 262176 | tf_op jit(solution)/shard_map/ppermute | solution.py:180
  57.5 6.3 %all-to-all-start = ((bf16[32,8,1024]{2,1,0:T(8,128)(2,1)}), bf16[32,8,1024]{2,1,0:T(8,128)(2,1)S(1)}, u32[]{:S(2)}, u32[]{:S(2)}) async-start(bf16[32,8,1024]{2,1,0:T(8,128)(2,1)} %fusion), calls=%async_computation | async-start | bytes 1048576 | tf_op jit(solution)/shard_map/all_to_all | solution.py:215
  64.2 3.0 %collective-permute-start.8 = (bf16[2048,128]{1,0:T(8,128)(2,1)S(1)}, bf16[2048,128]{1,0:T(8,128)(2,1)S(1)}, u32[]{:S(2)}, u32[]{:S(2)}) collective-permute-start(bf16[2048,128]{1,0:T(8,128)(2,1)S(1)} %bitcast.33), channel_id=1, source_target_pairs={{0,24},{8,0},{16,8},{24,16},{32,56},{40,32},{48,40},{56,48},{64,88... | collective-permute-start | bytes 1572872 | tf_op jit(solution)/shard_map/ppermute | solution.py:180
  67.3 2.8 %collective-permute-start.5 = (bf16[1024,128]{1,0:T(8,128)(2,1)}, bf16[1024,128]{1,0:T(8,128)(2,1)}, u32[]{:S(2)}, u32[]{:S(2)}) collective-permute-start(bf16[1024,128]{1,0:T(8,128)(2,1)} %collective-permute-done.4.refs_7_), channel_id=1, source_target_pairs={{0,224},{8,232},{16,240},{24,248},{32,0},{40,8},{48,16},{56,24},{6... | collective-permute-start | bytes 786440 | tf_op jit(solution)/shard_map/ppermute | solution.py:180
  70.6 11.7 %collective-permute-done.5.refs_6_ = bf16[1024,128]{1,0:T(8,128)(2,1)} collective-permute-done((bf16[1024,128]{1,0:T(8,128)(2,1)}, bf16[1024,128]{1,0:T(8,128)(2,1)}, u32[]{:S(2)}, u32[]{:S(2)}) %collective-permute-start.5) | collective-permute-done | bytes 262176 | tf_op jit(solution)/shard_map/ppermute | solution.py:180
  84.3 2.8 %collective-permute-start.10 = (bf16[1024,128]{1,0:T(8,128)(2,1)S(1)}, bf16[1024,128]{1,0:T(8,128)(2,1)}, u32[]{:S(2)}, u32[]{:S(2)}) collective-permute-start(bf16[1024,128]{1,0:T(8,128)(2,1)S(1)} %slice.9), channel_id=1, source_target_pairs={{0,24},{8,0},{16,8},{24,16},{32,56},{40,32},{48,40},{56,48},{64,88... | collective-permute-start | bytes 786440 | tf_op jit(solution)/shard_map/ppermute | solution.py:180
  92.2 2.9 %collective-permute-done.9.refs_11_ = bf16[1024,128]{1,0:T(8,128)(2,1)} collective-permute-done((bf16[1024,128]{1,0:T(8,128)(2,1)S(1)}, bf16[1024,128]{1,0:T(8,128)(2,1)}, u32[]{:S(2)}, u32[]{:S(2)}) %collective-permute-start.9) | collective-permute-done | bytes 262176 | tf_op jit(solution)/shard_map/ppermute | solution.py:180
  95.1 41.1 %attend.1 = (bf16[256,1024]{1,0:T(8,128)(2,1)}, bf16[256,1024]{1,0:T(8,128)(2,1)}, bf16[1024,128]{1,0:T(8,128)(2,1)}, bf16[1024,128]{1,0:T(8,128)(2,1)}, bf16[10...) custom-call(s32[8]{0:T(128)} %get-tuple-element.42.lo_ref, ...), custom_call_target="tpu_custom_call" | custom-call | flops 12000000000 | bytes 12000000 | tf_op jit(solution)/shard_map/attend/pallas_call | solution.py:152
  139.5 5.0 %all-to-all-start.4 = ((bf16[8,32,1024]{2,1,0:T(8,128)(2,1)}), bf16[8,32,1024]{2,1,0:T(8,128)(2,1)S(1)}, u32[]{:S(2)}, u32[]{:S(2)}) async-start(bf16[8,32,1024]{2,1,0:T(8,128)(2,1)} %bitcast.37), calls=%async_computation.4 | async-start | bytes 1048576 | tf_op jit(solution)/shard_map/all_to_all | solution.py:246
  146.6 3.2 %collective-permute-start.22 = (bf16[1024,128]{1,0:T(8,128)(2,1)S(1)}, bf16[1024,128]{1,0:T(8,128)(2,1)S(1)}, u32[]{:S(2)}, u32[]{:S(2)}) collective-permute-start(bf16[1024,128]{1,0:T(8,128)(2,1)S(1)} %copy-done.22), channel_id=1, source_target_pairs={{0,24},{8,0},{16,8},{24,16},{32,56},{40,32},{48,40},{56,48},{64,88... | collective-permute-start | bytes 786440 | tf_op jit(solution)/shard_map/ppermute | solution.py:180
  151.1 3.9 %collective-permute-done.19 = bf16[1024,128]{1,0:T(8,128)(2,1)S(1)} collective-permute-done((bf16[1024,128]{1,0:T(8,128)(2,1)S(1)}, bf16[1024,128]{1,0:T(8,128)(2,1)S(1)}, u32[]{:S(2)}, u32[]{:S(2)}) %collective-permute-start.19) | collective-permute-done | bytes 262176 | tf_op jit(solution)/shard_map/ppermute | solution.py:180
  159.8 9.6 %all-to-all-start.5 = ((bf16[32,8,1024]{2,1,0:T(8,128)(2,1)}), bf16[32,8,1024]{2,1,0:T(8,128)(2,1)S(1)}, u32[]{:S(2)}, u32[]{:S(2)}) async-start(bf16[32,8,1024]{2,1,0:T(8,128)(2,1)} %bitcast.11), calls=%async_computation.5 | async-start | bytes 1048576 | tf_op jit(solution)/shard_map/all_to_all | solution.py:245
  169.5 3.3 %collective-permute-start.23 = (bf16[1024,128]{1,0:T(8,128)(2,1)S(1)}, bf16[1024,128]{1,0:T(8,128)(2,1)S(1)}, u32[]{:S(2)}, u32[]{:S(2)}) collective-permute-start(bf16[1024,128]{1,0:T(8,128)(2,1)S(1)} %add_convert_fusion.1), channel_id=1, source_target_pairs={{0,24},{8,0},{16,8},{24,16},{32,56},{40,32},{48,40},{56,48},{64,88... | collective-permute-start | bytes 786440 | tf_op jit(solution)/shard_map/ppermute | solution.py:180
  172.9 2.8 %collective-permute-start.17 = (bf16[1024,128]{1,0:T(8,128)(2,1)S(1)}, bf16[1024,128]{1,0:T(8,128)(2,1)S(1)}, u32[]{:S(2)}, u32[]{:S(2)}) collective-permute-start(bf16[1024,128]{1,0:T(8,128)(2,1)S(1)} %add_convert_fusion.5), channel_id=1, source_target_pairs={{0,224},{8,232},{16,240},{24,248},{32,0},{40,8},{48,16},{56,24},{6... | collective-permute-start | bytes 786440 | tf_op jit(solution)/shard_map/ppermute | solution.py:180
  177.9 2.3 %collective-permute-done.23 = bf16[1024,128]{1,0:T(8,128)(2,1)S(1)} collective-permute-done((bf16[1024,128]{1,0:T(8,128)(2,1)S(1)}, bf16[1024,128]{1,0:T(8,128)(2,1)S(1)}, u32[]{:S(2)}, u32[]{:S(2)}) %collective-permute-start.23) | collective-permute-done | bytes 262176 | tf_op jit(solution)/shard_map/ppermute | solution.py:180
  181.2 5.2 %collective-permute-done.17 = bf16[1024,128]{1,0:T(8,128)(2,1)S(1)} collective-permute-done((bf16[1024,128]{1,0:T(8,128)(2,1)S(1)}, bf16[1024,128]{1,0:T(8,128)(2,1)S(1)}, u32[]{:S(2)}, u32[]{:S(2)}) %collective-permute-start.17) | collective-permute-done | bytes 262176 | tf_op jit(solution)/shard_map/ppermute | solution.py:180
  188.5 4.3 %all-to-all-start.6 = ((bf16[4,256,128]{2,1,0:T(8,128)(2,1)}), bf16[4,256,128]{2,1,0:T(8,128)(2,1)S(1)}, u32[]{:S(2)}, u32[]{:S(2)}) async-start(bf16[4,256,128]{2,1,0:T(8,128)(2,1)} %bitcast.13), calls=%async_computation.6 | async-start | bytes 524288 | tf_op jit(solution)/shard_map/all_to_all | solution.py:188
  193.6 5.8 %all-to-all-done.6 = bf16[4,256,128]{2,1,0:T(8,128)(2,1)S(1)} async-done(((bf16[4,256,128]{2,1,0:T(8,128)(2,1)}), bf16[4,256,128]{2,1,0:T(8,128)(2,1)S(1)}, u32[]{:S(2)}, u32[]{:S(2)}) %all-to-all-start.6) | async-done | bytes 262176 | tf_op jit(solution)/shard_map/all_to_all | solution.py:188
  199.5 4.5 %all-to-all-start.7 = ((bf16[8,256,128]{2,1,0:T(8,128)(2,1)}), bf16[8,256,128]{2,1,0:T(8,128)(2,1)S(1)}, u32[]{:S(2)}, u32[]{:S(2)}) async-start(bf16[8,256,128]{2,1,0:T(8,128)(2,1)} %bitcast.14), calls=%async_computation.7 | async-start | bytes 1048576 | tf_op jit(solution)/shard_map/all_to_all | solution.py:188
  206.6 12.4 %all-to-all-done.7 = bf16[8,256,128]{2,1,0:T(8,128)(2,1)S(1)} async-done(((bf16[8,256,128]{2,1,0:T(8,128)(2,1)}), bf16[8,256,128]{2,1,0:T(8,128)(2,1)S(1)}, u32[]{:S(2)}, u32[]{:S(2)}) %all-to-all-start.7) | async-done | bytes 524320 | tf_op jit(solution)/shard_map/all_to_all | solution.py:188
  (135 shorter events, 37.1 us)
Async XLA Ops:
  2.3 11.1 %all-to-all-start.2 = ((bf16[4,256,128]{2,1,0:T(8,128)(2,1)}), bf16[4,256,128]{2,1,0:T(8,128)(2,1)S(1)}, u32[]{:S(2)}, u32[]{:S(2)}) async-start(bf16[4,256,128]{2,1,0:T(8,128)(2,1)} %broadcast_in_dim.64), calls=%async_computation.2 | async-start | bytes 524288 | tf_op jit(solution)/shard_map/all_to_all | solution.py:188
  28.1 28.7 %all-to-all-start.3 = ((bf16[8,256,128]{2,1,0:T(8,128)(2,1)}), bf16[8,256,128]{2,1,0:T(8,128)(2,1)S(1)}, u32[]{:S(2)}, u32[]{:S(2)}) async-start(bf16[8,256,128]{2,1,0:T(8,128)(2,1)} %broadcast_in_dim.65), calls=%async_computation.3 | async-start | bytes 1048576 | tf_op jit(solution)/shard_map/all_to_all | solution.py:188
  37.1 19.7 %collective-permute-start = (bf16[1024,128]{1,0:T(8,128)(2,1)S(1)}, bf16[1024,128]{1,0:T(8,128)(2,1)S(1)}, u32[]{:S(2)}, u32[]{:S(2)}) collective-permute-start(bf16[1024,128]{1,0:T(8,128)(2,1)S(1)} %bitcast.39), channel_id=1, source_target_pairs={{0,32},{8,40},{16,48},{24,56},{32,64},{40,72},{48,80},{56,88},{64,... | collective-permute-start | bytes 786440 | tf_op jit(solution)/shard_map/ppermute | solution.py:180
  40.3 26.9 %collective-permute-start.4 = (bf16[1024,128]{1,0:T(8,128)(2,1)S(1)}, bf16[1024,128]{1,0:T(8,128)(2,1)}, u32[]{:S(2)}, u32[]{:S(2)}) collective-permute-start(bf16[1024,128]{1,0:T(8,128)(2,1)S(1)} %bitcast.40), channel_id=1, source_target_pairs={{0,224},{8,232},{16,240},{24,248},{32,0},{40,8},{48,16},{56,24},{6... | collective-permute-start | bytes 786440 | tf_op jit(solution)/shard_map/ppermute | solution.py:180
  56.8 13.3 %collective-permute-start.1 = (bf16[1024,128]{1,0:T(8,128)(2,1)S(1)}, bf16[1024,128]{1,0:T(8,128)(2,1)}, u32[]{:S(2)}, u32[]{:S(2)}) collective-permute-start(bf16[1024,128]{1,0:T(8,128)(2,1)S(1)} %collective-permute-done.refs_1_), channel_id=1, source_target_pairs={{0,32},{8,40},{16,48},{24,56},{32,64},{40,72},{48,80},{56,88},{64,... | collective-permute-start | bytes 786440 | tf_op jit(solution)/shard_map/ppermute | solution.py:180
  57.5 32.7 %all-to-all-start = ((bf16[32,8,1024]{2,1,0:T(8,128)(2,1)}), bf16[32,8,1024]{2,1,0:T(8,128)(2,1)S(1)}, u32[]{:S(2)}, u32[]{:S(2)}) async-start(bf16[32,8,1024]{2,1,0:T(8,128)(2,1)} %fusion), calls=%async_computation | async-start | bytes 1048576 | tf_op jit(solution)/shard_map/all_to_all | solution.py:215
  64.2 20.1 %collective-permute-start.8 = (bf16[2048,128]{1,0:T(8,128)(2,1)S(1)}, bf16[2048,128]{1,0:T(8,128)(2,1)S(1)}, u32[]{:S(2)}, u32[]{:S(2)}) collective-permute-start(bf16[2048,128]{1,0:T(8,128)(2,1)S(1)} %bitcast.33), channel_id=1, source_target_pairs={{0,24},{8,0},{16,8},{24,16},{32,56},{40,32},{48,40},{56,48},{64,88... | collective-permute-start | bytes 1572872 | tf_op jit(solution)/shard_map/ppermute | solution.py:180
  67.2 19.9 %collective-permute-start.7 = (bf16[2048,128]{1,0:T(8,128)(2,1)S(1)}, bf16[2048,128]{1,0:T(8,128)(2,1)S(1)}, u32[]{:S(2)}, u32[]{:S(2)}) collective-permute-start(bf16[2048,128]{1,0:T(8,128)(2,1)S(1)} %bitcast.34), channel_id=1, source_target_pairs={{0,8},{8,16},{16,24},{24,0},{32,40},{40,48},{48,56},{56,32},{64,72... | collective-permute-start | bytes 1572872 | tf_op jit(solution)/shard_map/ppermute | solution.py:180
  67.3 15.0 %collective-permute-start.5 = (bf16[1024,128]{1,0:T(8,128)(2,1)}, bf16[1024,128]{1,0:T(8,128)(2,1)}, u32[]{:S(2)}, u32[]{:S(2)}) collective-permute-start(bf16[1024,128]{1,0:T(8,128)(2,1)} %collective-permute-done.4.refs_7_), channel_id=1, source_target_pairs={{0,224},{8,232},{16,240},{24,248},{32,0},{40,8},{48,16},{56,24},{6... | collective-permute-start | bytes 786440 | tf_op jit(solution)/shard_map/ppermute | solution.py:180
  70.1 13.8 %collective-permute-start.2 = (bf16[1024,128]{1,0:T(8,128)(2,1)}, bf16[1024,128]{1,0:T(8,128)(2,1)S(1)}, u32[]{:S(2)}, u32[]{:S(2)}) collective-permute-start(bf16[1024,128]{1,0:T(8,128)(2,1)} %collective-permute-done.1.refs_2_), channel_id=1, source_target_pairs={{0,32},{8,40},{16,48},{24,56},{32,64},{40,72},{48,80},{56,88},{64,... | collective-permute-start | bytes 786440 | tf_op jit(solution)/shard_map/ppermute | solution.py:180
  137.7 12.1 %collective-permute-start.15 = (bf16[1024,128]{1,0:T(8,128)(2,1)}, bf16[1024,128]{1,0:T(8,128)(2,1)S(1)}, u32[]{:S(2)}, u32[]{:S(2)}) collective-permute-start(bf16[1024,128]{1,0:T(8,128)(2,1)} %get-tuple-element.31), channel_id=1, source_target_pairs={{0,224},{8,232},{16,240},{24,248},{32,0},{40,8},{48,16},{56,24},{6... | collective-permute-start | bytes 786440 | tf_op jit(solution)/shard_map/ppermute | solution.py:180
  139.5 20.3 %all-to-all-start.4 = ((bf16[8,32,1024]{2,1,0:T(8,128)(2,1)}), bf16[8,32,1024]{2,1,0:T(8,128)(2,1)S(1)}, u32[]{:S(2)}, u32[]{:S(2)}) async-start(bf16[8,32,1024]{2,1,0:T(8,128)(2,1)} %bitcast.37), calls=%async_computation.4 | async-start | bytes 1048576 | tf_op jit(solution)/shard_map/all_to_all | solution.py:246
  144.5 31.3 %collective-permute-start.18 = (bf16[1024,128]{1,0:T(8,128)(2,1)}, bf16[1024,128]{1,0:T(8,128)(2,1)}, u32[]{:S(2)}, u32[]{:S(2)}) collective-permute-start(bf16[1024,128]{1,0:T(8,128)(2,1)} %get-tuple-element.33), channel_id=1, source_target_pairs={{0,24},{8,0},{16,8},{24,16},{32,56},{40,32},{48,40},{56,48},{64,88... | collective-permute-start | bytes 786440 | tf_op jit(solution)/shard_map/ppermute | solution.py:180
  146.5 31.3 %collective-permute-start.21 = (bf16[1024,128]{1,0:T(8,128)(2,1)}, bf16[1024,128]{1,0:T(8,128)(2,1)}, u32[]{:S(2)}, u32[]{:S(2)}) collective-permute-start(bf16[1024,128]{1,0:T(8,128)(2,1)} %get-tuple-element.37), channel_id=1, source_target_pairs={{0,8},{8,16},{16,24},{24,0},{32,40},{40,48},{48,56},{56,32},{64,72... | collective-permute-start | bytes 786440 | tf_op jit(solution)/shard_map/ppermute | solution.py:180
  146.6 12.1 %collective-permute-start.22 = (bf16[1024,128]{1,0:T(8,128)(2,1)S(1)}, bf16[1024,128]{1,0:T(8,128)(2,1)S(1)}, u32[]{:S(2)}, u32[]{:S(2)}) collective-permute-start(bf16[1024,128]{1,0:T(8,128)(2,1)S(1)} %copy-done.22), channel_id=1, source_target_pairs={{0,24},{8,0},{16,8},{24,16},{32,56},{40,32},{48,40},{56,48},{64,88... | collective-permute-start | bytes 786440 | tf_op jit(solution)/shard_map/ppermute | solution.py:180
  155.0 14.5 %collective-permute-start.16 = (bf16[1024,128]{1,0:T(8,128)(2,1)S(1)}, bf16[1024,128]{1,0:T(8,128)(2,1)S(1)}, u32[]{:S(2)}, u32[]{:S(2)}) collective-permute-start(bf16[1024,128]{1,0:T(8,128)(2,1)S(1)} %add_convert_fusion.6), channel_id=1, source_target_pairs={{0,224},{8,232},{16,240},{24,248},{32,0},{40,8},{48,16},{56,24},{6... | collective-permute-start | bytes 786440 | tf_op jit(solution)/shard_map/ppermute | solution.py:180
  158.4 17.5 %collective-permute-start.20 = (bf16[1024,128]{1,0:T(8,128)(2,1)S(1)}, bf16[1024,128]{1,0:T(8,128)(2,1)}, u32[]{:S(2)}, u32[]{:S(2)}) collective-permute-start(bf16[1024,128]{1,0:T(8,128)(2,1)S(1)} %add_convert_fusion.3), channel_id=1, source_target_pairs={{0,8},{8,16},{16,24},{24,0},{32,40},{40,48},{48,56},{56,32},{64,72... | collective-permute-start | bytes 786440 | tf_op jit(solution)/shard_map/ppermute | solution.py:180
  158.7 14.2 %collective-permute-start.13 = (bf16[1024,128]{1,0:T(8,128)(2,1)S(1)}, bf16[1024,128]{1,0:T(8,128)(2,1)S(1)}, u32[]{:S(2)}, u32[]{:S(2)}) collective-permute-start(bf16[1024,128]{1,0:T(8,128)(2,1)S(1)} %add_convert_fusion.8), channel_id=1, source_target_pairs={{0,32},{8,40},{16,48},{24,56},{32,64},{40,72},{48,80},{56,88},{64,... | collective-permute-start | bytes 786440 | tf_op jit(solution)/shard_map/ppermute | solution.py:180
  159.8 28.7 %all-to-all-start.5 = ((bf16[32,8,1024]{2,1,0:T(8,128)(2,1)}), bf16[32,8,1024]{2,1,0:T(8,128)(2,1)S(1)}, u32[]{:S(2)}, u32[]{:S(2)}) async-start(bf16[32,8,1024]{2,1,0:T(8,128)(2,1)} %bitcast.11), calls=%async_computation.5 | async-start | bytes 1048576 | tf_op jit(solution)/shard_map/all_to_all | solution.py:245
  169.5 10.7 %collective-permute-start.23 = (bf16[1024,128]{1,0:T(8,128)(2,1)S(1)}, bf16[1024,128]{1,0:T(8,128)(2,1)S(1)}, u32[]{:S(2)}, u32[]{:S(2)}) collective-permute-start(bf16[1024,128]{1,0:T(8,128)(2,1)S(1)} %add_convert_fusion.1), channel_id=1, source_target_pairs={{0,24},{8,0},{16,8},{24,16},{32,56},{40,32},{48,40},{56,48},{64,88... | collective-permute-start | bytes 786440 | tf_op jit(solution)/shard_map/ppermute | solution.py:180
  172.9 13.6 %collective-permute-start.17 = (bf16[1024,128]{1,0:T(8,128)(2,1)S(1)}, bf16[1024,128]{1,0:T(8,128)(2,1)S(1)}, u32[]{:S(2)}, u32[]{:S(2)}) collective-permute-start(bf16[1024,128]{1,0:T(8,128)(2,1)S(1)} %add_convert_fusion.5), channel_id=1, source_target_pairs={{0,224},{8,232},{16,240},{24,248},{32,0},{40,8},{48,16},{56,24},{6... | collective-permute-start | bytes 786440 | tf_op jit(solution)/shard_map/ppermute | solution.py:180
  175.8 11.9 %collective-permute-start.14 = (bf16[1024,128]{1,0:T(8,128)(2,1)S(1)}, bf16[1024,128]{1,0:T(8,128)(2,1)S(1)}, u32[]{:S(2)}, u32[]{:S(2)}) collective-permute-start(bf16[1024,128]{1,0:T(8,128)(2,1)S(1)} %add_convert_fusion.7), channel_id=1, source_target_pairs={{0,32},{8,40},{16,48},{24,56},{32,64},{40,72},{48,80},{56,88},{64,... | collective-permute-start | bytes 786440 | tf_op jit(solution)/shard_map/ppermute | solution.py:180
  188.5 10.9 %all-to-all-start.6 = ((bf16[4,256,128]{2,1,0:T(8,128)(2,1)}), bf16[4,256,128]{2,1,0:T(8,128)(2,1)S(1)}, u32[]{:S(2)}, u32[]{:S(2)}) async-start(bf16[4,256,128]{2,1,0:T(8,128)(2,1)} %bitcast.13), calls=%async_computation.6 | async-start | bytes 524288 | tf_op jit(solution)/shard_map/all_to_all | solution.py:188
  199.5 19.5 %all-to-all-start.7 = ((bf16[8,256,128]{2,1,0:T(8,128)(2,1)}), bf16[8,256,128]{2,1,0:T(8,128)(2,1)S(1)}, u32[]{:S(2)}, u32[]{:S(2)}) async-start(bf16[8,256,128]{2,1,0:T(8,128)(2,1)} %bitcast.14), calls=%async_computation.7 | async-start | bytes 1048576 | tf_op jit(solution)/shard_map/all_to_all | solution.py:188
  (31 other events, 259.7 us)
where the time goes:
time: 224 us; the launch traced here: 220 us
  starting transfers between devices  75.7 us (34%)
  waiting for transfers between devices  71.2 us (32%)
  Pallas kernels  41.1 us (18%)
  blocking collectives  13.8 us (6%)
  other arithmetic  7.77 us (3%)
  local copies, waits for them, and re-layouts  6.99 us (3%)
  matrix products  2.25 us (1%)
    ppermute x24, waiting for transfers between devices, shift(): return lax.ppermute(x, 'ctx', pairs)  46.3 us
    pallas_call x1, Pallas kernels, attend(): pl.pallas_call(attend_kernel, in_specs=[sm] * 3 + [vm] * (4 + len(ks) + l...  41.1 us
    ppermute x24, starting transfers between devices, shift(): return lax.ppermute(x, 'ctx', pairs)  33 us
    all_to_all x4, waiting for transfers between devices, swap(): return lax.all_to_all(x, 'ctx', 0, 0, axis_index_groups=groups, tiled=True)  24.9 us
    all_to_all x4, starting transfers between devices, swap(): return lax.all_to_all(x, 'ctx', 0, 0, axis_index_groups=groups, tiled=True)  21.8 us
    all_to_all x1, blocking collectives, body(): lax.all_to_all(out_grads, 'head', split_axis=1, concat_axis=0, tiled=True)  13.8 us
    all_to_all x1, starting transfers between devices, body(): lax.all_to_all(dq.reshape(n, PIECE, width), 'ctx', 0, 0, tiled=True)  9.63 us
    all_to_all x1, starting transfers between devices, body(): lax.all_to_all(outgoing.reshape(n, PIECE, width), 'ctx', 0, 0, tiled=True)  6.3 us
  transfers between devices with their start and end apart: 31, of which 13 were waited for; matrix products, arithmetic and copies ran while one was open for 6% of the time, Pallas kernels for 0%

commit v1 on v0

v1 whole, which is shorter than its diff:
```python
import jax
import jax.numpy as jnp
from jax import lax
from jax.experimental import pallas as pl
from jax.experimental.pallas import tpu as pltpu
from jax.sharding import Mesh
from jax.sharding import PartitionSpec as P

HD = 128
NZ = 8
NY = 4
TOK = 256
PLANE = NY * TOK
PIECE = 8
DOCLEN = 4096
DOCS = 8
GROUPS = 8
MOST = DOCLEN // PLANE + 1
MASKED = -1e30
LOG2E = 1.4426950408889634
f32 = jnp.float32
bf16 = jnp.bfloat16


def attend_kernel(lo_ref, hi_ref, at_ref, place_ref, start_ref, q_ref, g_ref, *refs):
    own_refs, twin_refs = refs[:NZ], refs[NZ : 2 * NZ]
    refs = refs[2 * NZ :]
    o_ref, dq_ref = refs[:2]
    keep_refs, give_refs = refs[2 : 2 + NZ], refs[2 + NZ : 2 + 2 * NZ]
    kn, vn, kt, vt, dk_acc, dv_acc, s_ref, e_ref = refs[2 + 2 * NZ :]
    rows, width = q_ref.shape
    heads = width // HD
    span = rows // GROUPS
    lanes = span * heads
    scale = HD**-0.5
    half = PLANE // 2
    my_z = at_ref[0]

    for rz in range(NZ):
        z = lax.rem(my_z + NZ - rz, NZ)
        for part, refs_of in ((slice(0, half), own_refs), (slice(half, PLANE), twin_refs)):
            kn[z, part, :] = refs_of[rz][:, :HD]
            vn[z, part, :] = refs_of[rz][:, HD:]

    def prepare(b, carry):
        kt[b] = kn[b].T
        vt[b] = vn[b].T
        dk_acc[b] = jnp.zeros(dk_acc.shape[1:], f32)
        dv_acc[b] = jnp.zeros(dv_acc.shape[1:], f32)
        return carry

    lax.fori_loop(0, NZ, prepare, 0)

    def gather_heads(ref, at):
        x = ref[at, :]
        return jnp.concatenate([x[:, h * HD : (h + 1) * HD] for h in range(heads)], axis=0)

    def scatter_heads(ref, at, x):
        for h in range(heads):
            ref[at, h * HD : (h + 1) * HD] = x[h * span : (h + 1) * span]

    def group(gi, carry):
        at = pl.ds(pl.multiple_of(gi * span, span), span)
        lo, hi = lo_ref[gi], hi_ref[gi]
        place, start = place_ref[gi], start_ref[gi]
        qt = gather_heads(q_ref, at).astype(f32).T
        gt = gather_heads(g_ref, at).astype(f32).T
        qtb, gtb = qt.astype(bf16), gt.astype(bf16)

        def score(kb, peak):
            s = jnp.dot(kn[kb], qtb, preferred_element_type=f32)
            u = lax.broadcasted_iota(jnp.int32, (TOK, lanes), 0)
            for ry in range(NY):
                base = kb * PLANE + at_ref[1 + ry] * TOK
                part = s[ry * TOK : (ry + 1) * TOK]
                part = jnp.where((u >= start - base) & (u <= place - base), part, MASKED)
                s_ref[kb - lo, ry * TOK : (ry + 1) * TOK, :] = part
                peak = jnp.maximum(peak, jnp.max(part.reshape(TOK // 8, 8, lanes), axis=0))
            return peak

        peak = lax.fori_loop(lo, hi, score, jnp.full((8, lanes), MASKED, f32))
        peak = jnp.max(peak, axis=0, keepdims=True) * (scale * LOG2E)

        def weigh(kb, carry):
            ot, total = carry
            e = jnp.exp2(s_ref[kb - lo] * (scale * LOG2E) - peak)
            eb = e.astype(bf16)
            e_ref[kb - lo] = eb
            total = total + jnp.sum(e.reshape(-1, 8, lanes), axis=0)
            return ot + jnp.dot(vt[kb], eb, preferred_element_type=f32), total

        ot, total = lax.fori_loop(
            lo, hi, weigh, (jnp.zeros((HD, lanes), f32), jnp.zeros((8, lanes), f32))
        )
        inverse = 1.0 / jnp.sum(total, axis=0, keepdims=True)
        otb = (ot * inverse).astype(bf16).astype(f32)
        scatter_heads(o_ref, at, otb.T.astype(bf16))
        delta = jnp.sum(otb * gt, axis=0, keepdims=True)
        qs = (qt * inverse).T.astype(bf16)
        gs = (gt * inverse).T.astype(bf16)

        def back(kb, dqt):
            dp = jnp.dot(vn[kb], gtb, preferred_element_type=f32)
            eb = e_ref[kb - lo]
            ds = (eb.astype(f32) * (dp - delta)).astype(bf16)
            dk_acc[kb] += jnp.dot(ds, qs, preferred_element_type=f32)
            dv_acc[kb] += jnp.dot(eb, gs, preferred_element_type=f32)
            return dqt + jnp.dot(kt[kb], ds, preferred_element_type=f32)

        dqt = lax.fori_loop(lo, hi, back, jnp.zeros((HD, lanes), f32))
        scatter_heads(dq_ref, at, (dqt * (inverse * scale)).T.astype(bf16))
        return carry

    lax.fori_loop(0, GROUPS, group, 0)

    for rz in range(NZ):
        z = lax.rem(my_z + rz, NZ)
        for part, refs_of in ((slice(0, half), keep_refs), (slice(half, PLANE), give_refs)):
            refs_of[rz][:, :HD] = (dk_acc[z, part, :] * scale).astype(bf16)
            refs_of[rz][:, HD:] = dv_acc[z, part, :].astype(bf16)


def attend(lo, hi, at, place, start, q, g, own, twin):
    rows, width = q.shape
    lanes = rows // GROUPS * (width // HD)
    vm = pl.BlockSpec(memory_space=pltpu.VMEM)
    sm = pl.BlockSpec(memory_space=pltpu.SMEM)
    outs = (
        [jax.ShapeDtypeStruct((rows, width), bf16)] * 2
        + [jax.ShapeDtypeStruct((PLANE // 2, 2 * HD), bf16)] * (2 * NZ)
    )
    out = pl.pallas_call(
        attend_kernel,
        in_specs=[sm] * 3 + [vm] * (4 + 2 * NZ),
        out_specs=[vm] * len(outs),
        out_shape=outs,
        scratch_shapes=[
            pltpu.VMEM((NZ, PLANE, HD), bf16),
            pltpu.VMEM((NZ, PLANE, HD), bf16),
            pltpu.VMEM((NZ, HD, PLANE), bf16),
            pltpu.VMEM((NZ, HD, PLANE), bf16),
            pltpu.VMEM((NZ, PLANE, HD), f32),
            pltpu.VMEM((NZ, PLANE, HD), f32),
            pltpu.VMEM((MOST, PLANE, lanes), f32),
            pltpu.VMEM((MOST, PLANE, lanes), bf16),
        ],
        compiler_params=pltpu.CompilerParams(vmem_limit_bytes=52 * 1024 * 1024),
        cost_estimate=pl.CostEstimate(
            flops=12 * 10**9, bytes_accessed=12 * 10**6, transcendentals=4 * 10**6
        ),
        name="attend",
    )(lo, hi, at, place, start, q, g, *own, *twin)
    return out[0], out[1], out[2 : 2 + NZ], out[2 + NZ :]


AXES = ("z", "p", "b", "x", "c")
OWNER = ("z", "p", "c")
HEAD = ("x", "b")


def swap(x):
    return lax.ppermute(x, ("b", "c"), [(0, 0), (1, 2), (2, 1), (3, 3)])


def ring(x, step):
    return lax.ppermute(x, "z", [(i, (i + step) % NZ) for i in range(NZ)])


def twin(x):
    return lax.ppermute(x, "c", [(0, 1), (1, 0)])


def across(x):
    return lax.ppermute(x, "p", [(0, 1), (1, 0)])


def after(x, *others):
    return lax.optimization_barrier((x, others))[0]


def add(*terms):
    total = terms[0].astype(f32)
    for x in terms[1:]:
        total = total + x.astype(f32)
    return total.astype(bf16)


def body(queries, key_rows, value_rows, out_grads, doc_ids, owner_plan):
    n = NZ * NY
    me = lax.axis_index(OWNER)
    p, c = lax.axis_index("p"), lax.axis_index("c")
    rows, width = queries.shape
    pieces = jnp.arange(n, dtype=jnp.int32)
    my_owners = lax.dynamic_index_in_dim(owner_plan, me, 0, keepdims=False)

    mine = swap(jnp.concatenate([key_rows, value_rows], axis=1))
    home = swap(queries)
    mine = jnp.concatenate([mine, across(mine)], axis=0)

    r = jnp.arange(rows, dtype=jnp.int32)
    owner_row = jnp.repeat(my_owners, PIECE) * PIECE + r % PIECE
    onehot = (r[:, None] == owner_row[None, :]).astype(bf16)
    outgoing = jnp.dot(onehot, home, preferred_element_type=f32).astype(bf16)

    q = lax.all_to_all(outgoing.reshape(n, PIECE, width), OWNER, 0, 0, tiled=True).reshape(rows, width)
    g = lax.all_to_all(after(swap(out_grads), q), HEAD, split_axis=1, concat_axis=0, tiled=True)

    ups, downs = [mine], [mine]
    for step in range(NZ // 2):
        ups.append(ring(ups[-1], 1))
        if step < NZ // 2 - 1:
            downs.append(ring(downs[-1], -1))
    own = ups + downs[:0:-1]
    twins = [twin(x) for x in own]

    slot_of = jnp.sum(jnp.where(owner_plan == me, pieces[None, :], 0), axis=1)
    place = (
        pieces[:, None] * TOK + slot_of[:, None] * PIECE + jnp.arange(PIECE, dtype=jnp.int32)[None, :]
    ).reshape(GROUPS, 1, 1, rows // GROUPS)
    docs = jnp.arange(DOCS, dtype=jnp.int32)
    doc_first = jnp.sum((doc_ids[:, None] < docs[None, :]).astype(jnp.int32), axis=0)
    start = jnp.max(jnp.where(doc_first <= place[..., None], doc_first, 0), axis=-1)
    lo = jnp.min(start, axis=(1, 2, 3)) // PLANE
    hi = jnp.max(place, axis=(1, 2, 3)) // PLANE + 1
    spread_lanes = lambda x: jnp.broadcast_to(x, (GROUPS, 1, width // HD, rows // GROUPS)).reshape(GROUPS, 1, -1)
    at = jnp.stack([me // NY] + [2 * (p ^ (j & 1)) + (c ^ (j >> 1)) for j in range(NY)])

    o, dq, keep, give = attend(lo, hi, at, spread_lanes(place), spread_lanes(start), q, g, own, twins)

    got = [None] * NZ
    for r in (4, 5, 3, 6, 2, 7, 1, 0):
        got[r] = twin(give[r])
    up = ring(add(keep[4], got[4]), 1)
    down = ring(add(keep[5], got[5]), -1)
    for r in (3, 2, 1):
        up = ring(add(keep[r], got[r], up), 1)
        if r > 1:
            down = ring(add(keep[9 - r], got[9 - r], down), -1)
    total = [x.astype(f32) for x in (keep[0], got[0], up, down)]
    total = total[0] + total[1] + total[2] + total[3]
    other = across(total[TOK:].astype(bf16))
    grads = swap((total[:TOK] + other.astype(f32)).astype(bf16))

    returned = lax.all_to_all(dq.reshape(n, PIECE, width), OWNER, 0, 0, tiled=True).reshape(rows, width)
    attention = lax.all_to_all(after(o, returned), HEAD, split_axis=0, concat_axis=1, tiled=True)
    query_grads = jnp.dot(onehot.T, returned, preferred_element_type=f32).astype(bf16)
    return swap(attention), swap(query_grads), grads[:, :HD], grads[:, HD:]


def solution(mesh):
    ctx, head = ("z", "p", "b"), ("x", "c")
    fine = Mesh(mesh.devices.reshape(NZ, 2, 2, -1, 2), AXES)
    rows = P(ctx + head, None)
    return jax.shard_map(
        body,
        mesh=fine,
        in_specs=(P(ctx, head),) * 3 + (rows, P(), P()),
        out_specs=(rows,) + (P(ctx, head),) * 3,
        check_vma=False,
    )
```

time: 224 us -> 197 us (0.88)
  the two profiles are of different devices: /device:TPU:2 before, /device:TPU:99 now
where the time goes in v1:
time: 197 us; the launch traced here: 196 us
  starting transfers between devices  84.1 us (43%)
  waiting for transfers between devices  57.9 us (29%)
  Pallas kernels  39.7 us (20%)
  other arithmetic  6.79 us (3%)
  local copies, waits for them, and re-layouts  5 us (3%)
    pallas_call x1, Pallas kernels, attend(): pl.pallas_call(attend_kernel, in_specs=[sm] * 3 + [vm] * (4 + 2 * NZ), ou...  39.7 us
    ppermute x14, waiting for transfers between devices, ring(): return lax.ppermute(x, 'z', [(i, (i + step) % NZ) for i in range(NZ)])  30.9 us
    ppermute x14, starting transfers between devices, ring(): return lax.ppermute(x, 'z', [(i, (i + step) % NZ) for i in range(NZ)])  19.7 us
    ppermute x2, waiting for transfers between devices, across(): return lax.ppermute(x, 'p', [(0, 1), (1, 0)])  19.1 us
    ppermute x6, starting transfers between devices, swap(): return lax.ppermute(x, ('b', 'c'), [(0, 0), (1, 2), (2, 1), (3, 3)])  17.7 us
    ppermute x16, starting transfers between devices, twin(): return lax.ppermute(x, 'c', [(0, 1), (1, 0)])  13 us
    all_to_all x1, starting transfers between devices, body(): lax.all_to_all(dq.reshape(n, PIECE, width), OWNER, 0, 0, tiled=True)  9.9 us
    ppermute x2, starting transfers between devices, across(): return lax.ppermute(x, 'p', [(0, 1), (1, 0)])  7.26 us
  transfers between devices with their start and end apart: 42, of which 13 were waited for; matrix products, arithmetic and copies ran while one was open for 5% of the time, Pallas kernels for 0%

profile of v1, /device:TPU:99, one launch (start us, length us, event | category | flops | bytes accessed | tf_op | source)
XLA Modules:
  0.0 196.1 jit_solution(2018736016911539421)
XLA Ops:
  1.5 3.8 %collective-permute-start.2 = (bf16[256,256]{1,0:T(8,128)(2,1)S(1)}, bf16[256,256]{1,0:T(8,128)(2,1)S(1)}, u32[]{:S(2)}, u32[]{:S(2)}) collective-permute-start(bf16[256,256]{1,0:T(8,128)(2,1)S(1)} %pad_maximum_fusion), channel_id=1, source_target_pairs={{0,0},{1,8},{8,1},{9,9},{2,2},{3,10},{10,3},{11,11},{4,4},{5,12},{... | collective-permute-start | bytes 393224 | tf_op jit(solution)/shard_map/ppermute | solution.py:162
  7.9 3.9 %collective-permute-start.3 = (bf16[256,256]{1,0:T(8,128)(2,1)S(1)}, bf16[256,256]{1,0:T(8,128)(2,1)S(1)}, u32[]{:S(2)}, u32[]{:S(2)}) collective-permute-start(bf16[256,256]{1,0:T(8,128)(2,1)S(1)} %collective-permute-done.2), channel_id=1, source_target_pairs={{0,16},{16,0},{1,17},{17,1},{2,18},{18,2},{3,19},{19,3},{4,20},{20... | collective-permute-start | bytes 393224 | tf_op jit(solution)/shard_map/ppermute | solution.py:174
  12.0 6.7 %collective-permute-done.3 = bf16[256,256]{1,0:T(8,128)(2,1)S(1)} collective-permute-done((bf16[256,256]{1,0:T(8,128)(2,1)S(1)}, bf16[256,256]{1,0:T(8,128)(2,1)S(1)}, u32[]{:S(2)}, u32[]{:S(2)}) %collective-permute-start.3) | collective-permute-done | bytes 131104 | tf_op jit(solution)/shard_map/ppermute | solution.py:174
  18.7 2.9 %collective-permute-start.4 = (bf16[512,256]{1,0:T(8,128)(2,1)S(1)}, bf16[512,256]{1,0:T(8,128)(2,1)S(1)}, u32[]{:S(2)}, u32[]{:S(2)}) collective-permute-start(bf16[512,256]{1,0:T(8,128)(2,1)S(1)} %constant_dynamic-update-slice_fusion.refs_0_), channel_id=1, source_target_pairs={{0,32},{32,64},{64,96},{96,128},{128,160},{160,192},{192,224},{224... | collective-permute-start | bytes 786440 | tf_op jit(solution)/shard_map/ppermute | solution.py:166
  22.7 6.4 %all-to-all-start = ((bf16[32,8,1024]{2,1,0:T(8,128)(2,1)}), bf16[32,8,1024]{2,1,0:T(8,128)(2,1)S(1)}, u32[]{:S(2)}, u32[]{:S(2)}) async-start(bf16[32,8,1024]{2,1,0:T(8,128)(2,1)} %fusion), calls=%async_computation | async-start | bytes 1048576 | tf_op jit(solution)/shard_map/all_to_all | solution.py:205
  29.5 2.4 %collective-permute-start.5 = (bf16[512,256]{1,0:T(8,128)(2,1)S(1)}, bf16[512,256]{1,0:T(8,128)(2,1)S(1)}, u32[]{:S(2)}, u32[]{:S(2)}) collective-permute-start(bf16[512,256]{1,0:T(8,128)(2,1)S(1)} %collective-permute-done.4.refs_1_), channel_id=1, source_target_pairs={{0,32},{32,64},{64,96},{96,128},{128,160},{160,192},{192,224},{224... | collective-permute-start | bytes 786440 | tf_op jit(solution)/shard_map/ppermute | solution.py:166
  31.9 4.2 %collective-permute-start.1 = (bf16[32,8192]{1,0:T(8,128)(2,1)S(1)}, bf16[32,8192]{1,0:T(8,128)(2,1)S(1)}, u32[]{:S(2)}, u32[]{:S(2)}) collective-permute-start(bf16[32,8192]{1,0:T(8,128)(2,1)S(1)} %copy-done.6), channel_id=1, source_target_pairs={{0,0},{1,8},{8,1},{9,9},{2,2},{3,10},{10,3},{11,11},{4,4},{5,12},{... | collective-permute-start | bytes 1572872 | tf_op jit(solution)/shard_map/ppermute | solution.py:162
  36.2 13.2 %collective-permute-done.8.refs_7_ = bf16[512,256]{1,0:T(8,128)(2,1)S(1)} collective-permute-done((bf16[512,256]{1,0:T(8,128)(2,1)S(1)}, bf16[512,256]{1,0:T(8,128)(2,1)S(1)}, u32[]{:S(2)}, u32[]{:S(2)}) %collective-permute-start.8) | collective-permute-done | bytes 262176 | tf_op jit(solution)/shard_map/ppermute | solution.py:166
  49.4 2.7 %collective-permute-start.6 = (bf16[512,256]{1,0:T(8,128)(2,1)S(1)}, bf16[512,256]{1,0:T(8,128)(2,1)}, u32[]{:S(2)}, u32[]{:S(2)}) collective-permute-start(bf16[512,256]{1,0:T(8,128)(2,1)S(1)} %collective-permute-done.5.refs_2_), channel_id=1, source_target_pairs={{0,32},{32,64},{64,96},{96,128},{128,160},{160,192},{192,224},{224... | collective-permute-start | bytes 786440 | tf_op jit(solution)/shard_map/ppermute | solution.py:166
  54.4 3.3 %collective-permute-done.9.refs_6_ = bf16[512,256]{1,0:T(8,128)(2,1)S(1)} collective-permute-done((bf16[512,256]{1,0:T(8,128)(2,1)S(1)}, bf16[512,256]{1,0:T(8,128)(2,1)S(1)}, u32[]{:S(2)}, u32[]{:S(2)}) %collective-permute-start.9) | collective-permute-done | bytes 262176 | tf_op jit(solution)/shard_map/ppermute | solution.py:166
  57.7 2.7 %collective-permute-start.7 = (bf16[512,256]{1,0:T(8,128)(2,1)}, bf16[512,256]{1,0:T(8,128)(2,1)}, u32[]{:S(2)}, u32[]{:S(2)}) collective-permute-start(bf16[512,256]{1,0:T(8,128)(2,1)} %collective-permute-done.6.refs_3_), channel_id=1, source_target_pairs={{0,32},{32,64},{64,96},{96,128},{128,160},{160,192},{192,224},{224... | collective-permute-start | bytes 786440 | tf_op jit(solution)/shard_map/ppermute | solution.py:166
  61.4 5.6 %all-to-all-start.1 = ((bf16[32,8,1024]{2,0,1:T(8,128)(2,1)}), bf16[32,8,1024]{2,0,1:T(8,128)(2,1)S(1)}, u32[]{:S(2)}, u32[]{:S(2)}) async-start(bf16[32,8,1024]{2,0,1:T(8,128)(2,1)} %bitcast.27), calls=%async_computation.1 | async-start | bytes 1048576 | tf_op jit(solution)/shard_map/all_to_all | solution.py:206
  67.3 2.8 %collective-permute-start.17 = (bf16[512,256]{1,0:T(8,128)(2,1)S(1)}, bf16[512,256]{1,0:T(8,128)(2,1)S(1)}, u32[]{:S(2)}, u32[]{:S(2)}) collective-permute-start(bf16[512,256]{1,0:T(8,128)(2,1)S(1)} %collective-permute-done.9.refs_6_), channel_id=1, source_target_pairs={{0,1},{1,0},{2,3},{3,2},{4,5},{5,4},{6,7},{7,6},{8,9},{9,8},{10,11... | collective-permute-start | bytes 786440 | tf_op jit(solution)/shard_map/ppermute | solution.py:170
  74.0 39.7 %attend.1 = (bf16[256,1024]{1,0:T(8,128)(2,1)}, bf16[256,1024]{1,0:T(8,128)(2,1)}, bf16[512,256]{1,0:T(8,128)(2,1)S(1)}, bf16[512,256]{1,0:T(8,128)(2,1)S(1)}, b...) custom-call(s32[8]{0:T(128)S(1)} %get-tuple-element.48.lo_ref, ...), custom_call_target="tpu_custom_call" | custom-call | flops 12000000000 | bytes 12000000 | tf_op jit(solution)/shard_map/attend/pallas_call | solution.py:132
  113.7 3.3 %collective-permute-start.25 = (bf16[512,256]{1,0:T(8,128)(2,1)}, bf16[512,256]{1,0:T(8,128)(2,1)S(1)}, u32[]{:S(2)}, u32[]{:S(2)}) collective-permute-start(bf16[512,256]{1,0:T(8,128)(2,1)} %get-tuple-element.37), channel_id=1, source_target_pairs={{0,1},{1,0},{2,3},{3,2},{4,5},{5,4},{6,7},{7,6},{8,9},{9,8},{10,11... | collective-permute-start | bytes 786440 | tf_op jit(solution)/shard_map/ppermute | solution.py:170
  118.5 4.6 %all-to-all-start.3 = ((bf16[8,32,1024]{2,1,0:T(8,128)(2,1)}), bf16[8,32,1024]{2,1,0:T(8,128)(2,1)S(1)}, u32[]{:S(2)}, u32[]{:S(2)}) async-start(bf16[8,32,1024]{2,1,0:T(8,128)(2,1)} %bitcast.12), calls=%async_computation.3 | async-start | bytes 1048576 | tf_op jit(solution)/shard_map/all_to_all | solution.py:245
  131.0 9.9 %all-to-all-start.2 = ((bf16[32,8,1024]{2,1,0:T(8,128)(2,1)}), bf16[32,8,1024]{2,1,0:T(8,128)(2,1)S(1)}, u32[]{:S(2)}, u32[]{:S(2)}) async-start(bf16[32,8,1024]{2,1,0:T(8,128)(2,1)} %bitcast.10), calls=%async_computation.2 | async-start | bytes 1048576 | tf_op jit(solution)/shard_map/all_to_all | solution.py:244
  143.9 2.7 %collective-permute-start.28 = (bf16[512,256]{1,0:T(8,128)(2,1)S(1)}, bf16[512,256]{1,0:T(8,128)(2,1)S(1)}, u32[]{:S(2)}, u32[]{:S(2)}) collective-permute-start(bf16[512,256]{1,0:T(8,128)(2,1)S(1)} %add_convert_fusion.4), channel_id=1, source_target_pairs={{0,32},{32,64},{64,96},{96,128},{128,160},{160,192},{192,224},{224... | collective-permute-start | bytes 786440 | tf_op jit(solution)/shard_map/ppermute | solution.py:166
  147.3 13.8 %collective-permute-done.34 = bf16[512,256]{1,0:T(8,128)(2,1)S(1)} collective-permute-done((bf16[512,256]{1,0:T(8,128)(2,1)S(1)}, bf16[512,256]{1,0:T(8,128)(2,1)S(1)}, u32[]{:S(2)}, u32[]{:S(2)}) %collective-permute-start.34) | collective-permute-done | bytes 262176 | tf_op jit(solution)/shard_map/ppermute | solution.py:166
  162.8 2.7 %collective-permute-start.29 = (bf16[512,256]{1,0:T(8,128)(2,1)}, bf16[512,256]{1,0:T(8,128)(2,1)S(1)}, u32[]{:S(2)}, u32[]{:S(2)}) collective-permute-start(bf16[512,256]{1,0:T(8,128)(2,1)} %add_convert_fusion.3), channel_id=1, source_target_pairs={{0,32},{32,64},{64,96},{96,128},{128,160},{160,192},{192,224},{224... | collective-permute-start | bytes 786440 | tf_op jit(solution)/shard_map/ppermute | solution.py:166
  165.5 3.7 %collective-permute-start.19 = (bf16[32,8192]{1,0:T(8,128)(2,1)S(1)}, bf16[32,8192]{1,0:T(8,128)(2,1)S(1)}, u32[]{:S(2)}, u32[]{:S(2)}) collective-permute-start(bf16[32,8192]{1,0:T(8,128)(2,1)S(1)} %bitcast.32), channel_id=1, source_target_pairs={{0,0},{1,8},{8,1},{9,9},{2,2},{3,10},{10,3},{11,11},{4,4},{5,12},{... | collective-permute-start | bytes 1572872 | tf_op jit(solution)/shard_map/ppermute | solution.py:162
  171.7 3.4 %collective-permute-start.36 = (bf16[256,256]{1,0:T(8,128)(2,1)S(1)}, bf16[256,256]{1,0:T(8,128)(2,1)S(1)}, u32[]{:S(2)}, u32[]{:S(2)}) collective-permute-start(bf16[256,256]{1,0:T(8,128)(2,1)S(1)} %slice.25), channel_id=1, source_target_pairs={{0,16},{16,0},{1,17},{17,1},{2,18},{18,2},{3,19},{19,3},{4,20},{20... | collective-permute-start | bytes 393224 | tf_op jit(solution)/shard_map/ppermute | solution.py:174
  175.1 12.4 %collective-permute-done.36 = bf16[256,256]{1,0:T(8,128)(2,1)S(1)} collective-permute-done((bf16[256,256]{1,0:T(8,128)(2,1)S(1)}, bf16[256,256]{1,0:T(8,128)(2,1)S(1)}, u32[]{:S(2)}, u32[]{:S(2)}) %collective-permute-start.36) | collective-permute-done | bytes 131104 | tf_op jit(solution)/shard_map/ppermute | solution.py:174
  189.7 4.1 %collective-permute-done.37 = bf16[256,256]{1,0:T(8,128)(2,1)S(1)} collective-permute-done((bf16[256,256]{1,0:T(8,128)(2,1)S(1)}, bf16[256,256]{1,0:T(8,128)(2,1)S(1)}, u32[]{:S(2)}, u32[]{:S(2)}) %collective-permute-start.37) | collective-permute-done | bytes 131104 | tf_op jit(solution)/shard_map/ppermute | solution.py:162
  (141 shorter events, 34.2 us)
Async XLA Ops:
  5.3 16.3 %collective-permute-start = (bf16[256,1024]{1,0:T(8,128)(2,1)}, bf16[256,1024]{1,0:T(8,128)(2,1)S(1)}, u32[]{:S(2)}, u32[]{:S(2)}) collective-permute-start(bf16[256,1024]{1,0:T(8,128)(2,1)} %param.6), channel_id=1, source_target_pairs={{0,0},{1,8},{8,1},{9,9},{2,2},{3,10},{10,3},{11,11},{4,4},{5,12},{... | collective-permute-start | bytes 1572872 | tf_op jit(solution)/shard_map/ppermute | solution.py:162
  22.7 37.7 %all-to-all-start = ((bf16[32,8,1024]{2,1,0:T(8,128)(2,1)}), bf16[32,8,1024]{2,1,0:T(8,128)(2,1)S(1)}, u32[]{:S(2)}, u32[]{:S(2)}) async-start(bf16[32,8,1024]{2,1,0:T(8,128)(2,1)} %fusion), calls=%async_computation | async-start | bytes 1048576 | tf_op jit(solution)/shard_map/all_to_all | solution.py:205
  29.2 20.2 %collective-permute-start.8 = (bf16[512,256]{1,0:T(8,128)(2,1)S(1)}, bf16[512,256]{1,0:T(8,128)(2,1)S(1)}, u32[]{:S(2)}, u32[]{:S(2)}) collective-permute-start(bf16[512,256]{1,0:T(8,128)(2,1)S(1)} %constant_dynamic-update-slice_fusion.refs_0_), channel_id=1, source_target_pairs={{0,224},{32,0},{64,32},{96,64},{128,96},{160,128},{192,160},{224,1... | collective-permute-start | bytes 786440 | tf_op jit(solution)/shard_map/ppermute | solution.py:166
  29.5 19.9 %collective-permute-start.5 = (bf16[512,256]{1,0:T(8,128)(2,1)S(1)}, bf16[512,256]{1,0:T(8,128)(2,1)S(1)}, u32[]{:S(2)}, u32[]{:S(2)}) collective-permute-start(bf16[512,256]{1,0:T(8,128)(2,1)S(1)} %collective-permute-done.4.refs_1_), channel_id=1, source_target_pairs={{0,32},{32,64},{64,96},{96,128},{128,160},{160,192},{192,224},{224... | collective-permute-start | bytes 786440 | tf_op jit(solution)/shard_map/ppermute | solution.py:166
  31.9 22.0 %collective-permute-start.1 = (bf16[32,8192]{1,0:T(8,128)(2,1)S(1)}, bf16[32,8192]{1,0:T(8,128)(2,1)S(1)}, u32[]{:S(2)}, u32[]{:S(2)}) collective-permute-start(bf16[32,8192]{1,0:T(8,128)(2,1)S(1)} %copy-done.6), channel_id=1, source_target_pairs={{0,0},{1,8},{8,1},{9,9},{2,2},{3,10},{10,3},{11,11},{4,4},{5,12},{... | collective-permute-start | bytes 1572872 | tf_op jit(solution)/shard_map/ppermute | solution.py:162
  52.5 14.8 %collective-permute-start.11 = (bf16[512,256]{1,0:T(8,128)(2,1)S(1)}, bf16[512,256]{1,0:T(8,128)(2,1)}, u32[]{:S(2)}, u32[]{:S(2)}) collective-permute-start(bf16[512,256]{1,0:T(8,128)(2,1)S(1)} %constant_dynamic-update-slice_fusion.refs_0_), channel_id=1, source_target_pairs={{0,1},{1,0},{2,3},{3,2},{4,5},{5,4},{6,7},{7,6},{8,9},{9,8},{10,11... | collective-permute-start | bytes 786440 | tf_op jit(solution)/shard_map/ppermute | solution.py:170
  53.9 16.3 %collective-permute-start.18 = (bf16[512,256]{1,0:T(8,128)(2,1)S(1)}, bf16[512,256]{1,0:T(8,128)(2,1)}, u32[]{:S(2)}, u32[]{:S(2)}) collective-permute-start(bf16[512,256]{1,0:T(8,128)(2,1)S(1)} %collective-permute-done.8.refs_7_), channel_id=1, source_target_pairs={{0,1},{1,0},{2,3},{3,2},{4,5},{5,4},{6,7},{7,6},{8,9},{9,8},{10,11... | collective-permute-start | bytes 786440 | tf_op jit(solution)/shard_map/ppermute | solution.py:170
  54.0 16.3 %collective-permute-start.12 = (bf16[512,256]{1,0:T(8,128)(2,1)S(1)}, bf16[512,256]{1,0:T(8,128)(2,1)S(1)}, u32[]{:S(2)}, u32[]{:S(2)}) collective-permute-start(bf16[512,256]{1,0:T(8,128)(2,1)S(1)} %collective-permute-done.4.refs_1_), channel_id=1, source_target_pairs={{0,1},{1,0},{2,3},{3,2},{4,5},{5,4},{6,7},{7,6},{8,9},{9,8},{10,11... | collective-permute-start | bytes 786440 | tf_op jit(solution)/shard_map/ppermute | solution.py:170
  57.7 13.0 %collective-permute-start.10 = (bf16[512,256]{1,0:T(8,128)(2,1)S(1)}, bf16[512,256]{1,0:T(8,128)(2,1)S(1)}, u32[]{:S(2)}, u32[]{:S(2)}) collective-permute-start(bf16[512,256]{1,0:T(8,128)(2,1)S(1)} %collective-permute-done.9.refs_6_), channel_id=1, source_target_pairs={{0,224},{32,0},{64,32},{96,64},{128,96},{160,128},{192,160},{224,1... | collective-permute-start | bytes 786440 | tf_op jit(solution)/shard_map/ppermute | solution.py:166
  57.7 13.1 %collective-permute-start.7 = (bf16[512,256]{1,0:T(8,128)(2,1)}, bf16[512,256]{1,0:T(8,128)(2,1)}, u32[]{:S(2)}, u32[]{:S(2)}) collective-permute-start(bf16[512,256]{1,0:T(8,128)(2,1)} %collective-permute-done.6.refs_3_), channel_id=1, source_target_pairs={{0,32},{32,64},{64,96},{96,128},{128,160},{160,192},{192,224},{224... | collective-permute-start | bytes 786440 | tf_op jit(solution)/shard_map/ppermute | solution.py:166
  61.4 11.8 %all-to-all-start.1 = ((bf16[32,8,1024]{2,0,1:T(8,128)(2,1)}), bf16[32,8,1024]{2,0,1:T(8,128)(2,1)S(1)}, u32[]{:S(2)}, u32[]{:S(2)}) async-start(bf16[32,8,1024]{2,0,1:T(8,128)(2,1)} %bitcast.27), calls=%async_computation.1 | async-start | bytes 1048576 | tf_op jit(solution)/shard_map/all_to_all | solution.py:206
  118.5 12.5 %all-to-all-start.3 = ((bf16[8,32,1024]{2,1,0:T(8,128)(2,1)}), bf16[8,32,1024]{2,1,0:T(8,128)(2,1)S(1)}, u32[]{:S(2)}, u32[]{:S(2)}) async-start(bf16[8,32,1024]{2,1,0:T(8,128)(2,1)} %bitcast.12), calls=%async_computation.3 | async-start | bytes 1048576 | tf_op jit(solution)/shard_map/all_to_all | solution.py:245
  123.1 19.7 %collective-permute-start.23 = (bf16[512,256]{1,0:T(8,128)(2,1)}, bf16[512,256]{1,0:T(8,128)(2,1)S(1)}, u32[]{:S(2)}, u32[]{:S(2)}) collective-permute-start(bf16[512,256]{1,0:T(8,128)(2,1)} %get-tuple-element.33), channel_id=1, source_target_pairs={{0,1},{1,0},{2,3},{3,2},{4,5},{5,4},{6,7},{7,6},{8,9},{9,8},{10,11... | collective-permute-start | bytes 786440 | tf_op jit(solution)/shard_map/ppermute | solution.py:170
  124.1 16.9 %collective-permute-start.31 = (bf16[512,256]{1,0:T(8,128)(2,1)}, bf16[512,256]{1,0:T(8,128)(2,1)S(1)}, u32[]{:S(2)}, u32[]{:S(2)}) collective-permute-start(bf16[512,256]{1,0:T(8,128)(2,1)} %get-tuple-element.41), channel_id=1, source_target_pairs={{0,1},{1,0},{2,3},{3,2},{4,5},{5,4},{6,7},{7,6},{8,9},{9,8},{10,11... | collective-permute-start | bytes 786440 | tf_op jit(solution)/shard_map/ppermute | solution.py:170
  124.1 17.3 %collective-permute-start.33 = (bf16[512,256]{1,0:T(8,128)(2,1)S(1)}, bf16[512,256]{1,0:T(8,128)(2,1)}, u32[]{:S(2)}, u32[]{:S(2)}) collective-permute-start(bf16[512,256]{1,0:T(8,128)(2,1)S(1)} %add_convert_fusion.2), channel_id=1, source_target_pairs={{0,224},{32,0},{64,32},{96,64},{128,96},{160,128},{192,160},{224,1... | collective-permute-start | bytes 786440 | tf_op jit(solution)/shard_map/ppermute | solution.py:166
  127.3 15.5 %collective-permute-start.27 = (bf16[512,256]{1,0:T(8,128)(2,1)S(1)}, bf16[512,256]{1,0:T(8,128)(2,1)}, u32[]{:S(2)}, u32[]{:S(2)}) collective-permute-start(bf16[512,256]{1,0:T(8,128)(2,1)S(1)} %add_convert_fusion.5), channel_id=1, source_target_pairs={{0,32},{32,64},{64,96},{96,128},{128,160},{160,192},{192,224},{224... | collective-permute-start | bytes 786440 | tf_op jit(solution)/shard_map/ppermute | solution.py:166
  128.6 33.4 %collective-permute-start.22 = (bf16[512,256]{1,0:T(8,128)(2,1)}, bf16[512,256]{1,0:T(8,128)(2,1)S(1)}, u32[]{:S(2)}, u32[]{:S(2)}) collective-permute-start(bf16[512,256]{1,0:T(8,128)(2,1)} %get-tuple-element.31), channel_id=1, source_target_pairs={{0,1},{1,0},{2,3},{3,2},{4,5},{5,4},{6,7},{7,6},{8,9},{9,8},{10,11... | collective-permute-start | bytes 786440 | tf_op jit(solution)/shard_map/ppermute | solution.py:170
  131.0 38.2 %all-to-all-start.2 = ((bf16[32,8,1024]{2,1,0:T(8,128)(2,1)}), bf16[32,8,1024]{2,1,0:T(8,128)(2,1)S(1)}, u32[]{:S(2)}, u32[]{:S(2)}) async-start(bf16[32,8,1024]{2,1,0:T(8,128)(2,1)} %bitcast.10), calls=%async_computation.2 | async-start | bytes 1048576 | tf_op jit(solution)/shard_map/all_to_all | solution.py:244
  142.4 18.7 %collective-permute-start.34 = (bf16[512,256]{1,0:T(8,128)(2,1)S(1)}, bf16[512,256]{1,0:T(8,128)(2,1)S(1)}, u32[]{:S(2)}, u32[]{:S(2)}) collective-permute-start(bf16[512,256]{1,0:T(8,128)(2,1)S(1)} %add_convert_fusion.1), channel_id=1, source_target_pairs={{0,224},{32,0},{64,32},{96,64},{128,96},{160,128},{192,160},{224,1... | collective-permute-start | bytes 786440 | tf_op jit(solution)/shard_map/ppermute | solution.py:166
  143.9 18.1 %collective-permute-start.28 = (bf16[512,256]{1,0:T(8,128)(2,1)S(1)}, bf16[512,256]{1,0:T(8,128)(2,1)S(1)}, u32[]{:S(2)}, u32[]{:S(2)}) collective-permute-start(bf16[512,256]{1,0:T(8,128)(2,1)S(1)} %add_convert_fusion.4), channel_id=1, source_target_pairs={{0,32},{32,64},{64,96},{96,128},{128,160},{160,192},{192,224},{224... | collective-permute-start | bytes 786440 | tf_op jit(solution)/shard_map/ppermute | solution.py:166
  146.6 24.9 %collective-permute-start.21 = (bf16[512,256]{1,0:T(8,128)(2,1)}, bf16[512,256]{1,0:T(8,128)(2,1)S(1)}, u32[]{:S(2)}, u32[]{:S(2)}) collective-permute-start(bf16[512,256]{1,0:T(8,128)(2,1)} %get-tuple-element.29), channel_id=1, source_target_pairs={{0,1},{1,0},{2,3},{3,2},{4,5},{5,4},{6,7},{7,6},{8,9},{9,8},{10,11... | collective-permute-start | bytes 786440 | tf_op jit(solution)/shard_map/ppermute | solution.py:170
  165.5 24.2 %collective-permute-start.19 = (bf16[32,8192]{1,0:T(8,128)(2,1)S(1)}, bf16[32,8192]{1,0:T(8,128)(2,1)S(1)}, u32[]{:S(2)}, u32[]{:S(2)}) collective-permute-start(bf16[32,8192]{1,0:T(8,128)(2,1)S(1)} %bitcast.32), channel_id=1, source_target_pairs={{0,0},{1,8},{8,1},{9,9},{2,2},{3,10},{10,3},{11,11},{4,4},{5,12},{... | collective-permute-start | bytes 1572872 | tf_op jit(solution)/shard_map/ppermute | solution.py:162
  169.6 20.1 %collective-permute-start.20 = (bf16[256,1024]{1,0:T(8,128)(2,1)S(1)}, bf16[256,1024]{1,0:T(8,128)(2,1)S(1)}, u32[]{:S(2)}, u32[]{:S(2)}) collective-permute-start(bf16[256,1024]{1,0:T(8,128)(2,1)S(1)} %convolution_convert_fusion), channel_id=1, source_target_pairs={{0,0},{1,8},{8,1},{9,9},{2,2},{3,10},{10,3},{11,11},{4,4},{5,12},{... | collective-permute-start | bytes 1572872 | tf_op jit(solution)/shard_map/ppermute | solution.py:162
  171.7 15.8 %collective-permute-start.36 = (bf16[256,256]{1,0:T(8,128)(2,1)S(1)}, bf16[256,256]{1,0:T(8,128)(2,1)S(1)}, u32[]{:S(2)}, u32[]{:S(2)}) collective-permute-start(bf16[256,256]{1,0:T(8,128)(2,1)S(1)} %slice.25), channel_id=1, source_target_pairs={{0,16},{16,0},{1,17},{17,1},{2,18},{18,2},{3,19},{19,3},{4,20},{20... | collective-permute-start | bytes 393224 | tf_op jit(solution)/shard_map/ppermute | solution.py:174
  (35 other events, 279.1 us)

commit v2 on v1

--- a/solution.py
+++ b/solution.py
@@ -155,7 +155,6 @@
 
 AXES = ("z", "p", "b", "x", "c")
 OWNER = ("z", "p", "c")
-HEAD = ("x", "b")
 
 
 def swap(x):
@@ -170,12 +169,13 @@
     return lax.ppermute(x, "c", [(0, 1), (1, 0)])
 
 
-def across(x):
-    return lax.ppermute(x, "p", [(0, 1), (1, 0)])
-
-
-def after(x, *others):
-    return lax.optimization_barrier((x, others))[0]
+def swap_across(x):
+    pairs = [(4 * p + 2 * b + c, 4 * (1 - p) + 2 * c + b) for p in range(2) for b in range(2) for c in range(2)]
+    return lax.ppermute(x, ("p", "b", "c"), pairs)
+
+
+def nothing(x):
+    return x[0, 0].astype(f32) * 0.0
 
 
 def add(*terms):
@@ -191,20 +191,18 @@
     p, c = lax.axis_index("p"), lax.axis_index("c")
     rows, width = queries.shape
     pieces = jnp.arange(n, dtype=jnp.int32)
-    my_owners = lax.dynamic_index_in_dim(owner_plan, me, 0, keepdims=False)
-
-    mine = swap(jnp.concatenate([key_rows, value_rows], axis=1))
-    home = swap(queries)
-    mine = jnp.concatenate([mine, across(mine)], axis=0)
+    owners = lax.dynamic_index_in_dim(owner_plan, me, 0, keepdims=False)
 
     r = jnp.arange(rows, dtype=jnp.int32)
-    owner_row = jnp.repeat(my_owners, PIECE) * PIECE + r % PIECE
+    owner_row = jnp.repeat(owners, PIECE) * PIECE + r % PIECE
     onehot = (r[:, None] == owner_row[None, :]).astype(bf16)
-    outgoing = jnp.dot(onehot, home, preferred_element_type=f32).astype(bf16)
-
+    outgoing = jnp.dot(onehot, swap(queries), preferred_element_type=f32).astype(bf16)
     q = lax.all_to_all(outgoing.reshape(n, PIECE, width), OWNER, 0, 0, tiled=True).reshape(rows, width)
-    g = lax.all_to_all(after(swap(out_grads), q), HEAD, split_axis=1, concat_axis=0, tiled=True)
-
+    g = lax.all_to_all(out_grads, ("x", "c"), split_axis=1, concat_axis=0, tiled=True)
+    g = swap(g)
+
+    mine = jnp.concatenate([key_rows, value_rows], axis=1)
+    mine = jnp.concatenate([swap(mine), swap_across(mine)], axis=0)
     ups, downs = [mine], [mine]
     for step in range(NZ // 2):
         ups.append(ring(ups[-1], 1))
@@ -227,24 +225,24 @@
 
     o, dq, keep, give = attend(lo, hi, at, spread_lanes(place), spread_lanes(start), q, g, own, twins)
 
+    returned = lax.all_to_all(dq.reshape(n, PIECE, width), OWNER, 0, 0, tiled=True).reshape(rows, width)
+    o = swap(o)
+    attention = lax.all_to_all(add(o, nothing(returned)), ("x", "c"), split_axis=0, concat_axis=1, tiled=True)
+    query_grads = swap(jnp.dot(onehot.T, returned, preferred_element_type=f32).astype(bf16))
+
     got = [None] * NZ
     for r in (4, 5, 3, 6, 2, 7, 1, 0):
         got[r] = twin(give[r])
     up = ring(add(keep[4], got[4]), 1)
     down = ring(add(keep[5], got[5]), -1)
     for r in (3, 2, 1):
-        up = ring(add(keep[r], got[r], up), 1)
+        up = ring(add(keep[r], got[r], up, *([nothing(o)] if r == 2 else [])), 1)
         if r > 1:
             down = ring(add(keep[9 - r], got[9 - r], down), -1)
-    total = [x.astype(f32) for x in (keep[0], got[0], up, down)]
-    total = total[0] + total[1] + total[2] + total[3]
-    other = across(total[TOK:].astype(bf16))
-    grads = swap((total[:TOK] + other.astype(f32)).astype(bf16))
-
-    returned = lax.all_to_all(dq.reshape(n, PIECE, width), OWNER, 0, 0, tiled=True).reshape(rows, width)
-    attention = lax.all_to_all(after(o, returned), HEAD, split_axis=0, concat_axis=1, tiled=True)
-    query_grads = jnp.dot(onehot.T, returned, preferred_element_type=f32).astype(bf16)
-    return swap(attention), swap(query_grads), grads[:, :HD], grads[:, HD:]
+    total = add(keep[0], got[0], up, down, nothing(query_grads))
+    grads = add(swap(total[:TOK]), swap_across(total[TOK:]))
+
+    return attention, query_grads, grads[:, :HD], grads[:, HD:]
 
 
 def solution(mesh):

time: 197 us -> 178 us (0.904)
  waiting for transfers between devices: 57.9 us -> 40.7 us
  starting transfers between devices: 84.1 us -> 73.3 us
  local copies, waits for them, and re-layouts: 5 us -> 9.7 us
  between operations: 1.06 us -> 3.11 us
    ppermute x2, waiting for transfers between devices: 19.1 us -> 0.79 us  [swap_across(): return lax.ppermute(x, ('p', 'b', 'c'), pairs)]
    ppermute x16, starting transfers between devices: 13 us -> 5.3 us  [twin(): return lax.ppermute(x, 'c', [(0, 1), (1, 0)])]
    ppermute x14, waiting for transfers between devices: 30.9 us -> 36.3 us  [ring(): return lax.ppermute(x, 'z', [(i, (i + step) % NZ) for i in range(NZ)])]
    ppermute x6, waiting for transfers between devices: 4.78 us -> 0.69 us  [swap(): return lax.ppermute(x, ('b', 'c'), [(0, 0), (1, 2), (2, 1), (3, 3)])]
    convert_element_type x7 -> x10, other arithmetic: 5.02 us -> 7.8 us  [add(): return total.astype(bf16)]
    ppermute x2, starting transfers between devices: 7.26 us -> 4.64 us  [swap_across(): return lax.ppermute(x, ('p', 'b', 'c'), pairs)]
  transfers between devices with their start and end apart: 42 -> 42, of which waited for: 13 -> 12; matrix products, arithmetic and copies ran while one was open for 5% -> 9% of each run, Pallas kernels for 0% -> 0%
where the time goes in v2:
time: 178 us
  starting transfers between devices  73.3 us (41%)
  Pallas kernels  41.2 us (23%)
  waiting for transfers between devices  40.7 us (23%)
  local copies, waits for them, and re-layouts  9.7 us (5%)
  other arithmetic  8.53 us (5%)
  between operations  3.11 us (2%)
    pallas_call x1, Pallas kernels, attend(): pl.pallas_call(attend_kernel, in_specs=[sm] * 3 + [vm] * (4 + 2 * NZ), ou...  41.2 us
    ppermute x14, waiting for transfers between devices, ring(): return lax.ppermute(x, 'z', [(i, (i + step) % NZ) for i in range(NZ)])  36.3 us
    ppermute x14, starting transfers between devices, ring(): return lax.ppermute(x, 'z', [(i, (i + step) % NZ) for i in range(NZ)])  20.6 us
    ppermute x6, starting transfers between devices, swap(): return lax.ppermute(x, ('b', 'c'), [(0, 0), (1, 2), (2, 1), (3, 3)])  17.1 us
    all_to_all x1, starting transfers between devices, body(): lax.all_to_all(dq.reshape(n, PIECE, width), OWNER, 0, 0, tiled=True)  9.2 us
    convert_element_type x10, other arithmetic, add(): return total.astype(bf16)  7.8 us
    all_to_all x1, starting transfers between devices, body(): lax.all_to_all(add(o, nothing(returned)), ('x', 'c'), split_axis=0, conca...  6.36 us
    all_to_all x1, starting transfers between devices, body(): lax.all_to_all(outgoing.reshape(n, PIECE, width), OWNER, 0, 0, tiled=True)  5.43 us
  transfers between devices with their start and end apart: 42, of which 12 were waited for; matrix products, arithmetic and copies ran while one was open for 9% of the time, Pallas kernels for 0%

profile of v2, /device:TPU:99, one launch (start us, length us, event | category | flops | bytes accessed | tf_op | source)
XLA Modules:
  0.0 178.0 jit_solution(11412387298896689201)
XLA Ops:
  1.6 3.8 %collective-permute-start.2 = (bf16[256,256]{1,0:T(8,128)(2,1)S(1)}, bf16[256,256]{1,0:T(8,128)(2,1)S(1)}, u32[]{:S(2)}, u32[]{:S(2)}) collective-permute-start(bf16[256,256]{1,0:T(8,128)(2,1)S(1)} %constant_dynamic-update-slice_fusion), channel_id=1, source_target_pairs={{0,0},{1,8},{8,1},{9,9},{2,2},{3,10},{10,3},{11,11},{4,4},{5,12},{... | collective-permute-start | bytes 393224 | tf_op jit(solution)/shard_map/ppermute | solution.py:161
  7.0 1.9 %copy.20 = bf16[4,8,8,1024]{3,2,0,1:T(8,128)(2,1)} copy(bf16[4,8,8,1024]{3,2,1,0:T(8,128)(2,1)} %bitcast.33) | data formatting | bytes 1048576 | tf_op jit(solution)/shard_map/all_to_all | solution.py:201
  8.9 4.7 %all-to-all-start.1 = ((bf16[32,8,1024]{2,0,1:T(8,128)(2,1)}), bf16[32,8,1024]{2,0,1:T(8,128)(2,1)S(1)}, u32[]{:S(2)}, u32[]{:S(2)}) async-start(bf16[32,8,1024]{2,0,1:T(8,128)(2,1)} %bitcast.30), calls=%async_computation.1 | async-start | bytes 1048576 | tf_op jit(solution)/shard_map/all_to_all | solution.py:201
  13.6 3.1 %collective-permute-start = (bf16[256,1024]{1,0:T(8,128)(2,1)S(1)}, bf16[256,1024]{1,0:T(8,128)(2,1)S(1)}, u32[]{:S(2)}, u32[]{:S(2)}) collective-permute-start(bf16[256,1024]{1,0:T(8,128)(2,1)S(1)} %copy-done.6), channel_id=1, source_target_pairs={{0,0},{1,8},{8,1},{9,9},{2,2},{3,10},{10,3},{11,11},{4,4},{5,12},{... | collective-permute-start | bytes 1572872 | tf_op jit(solution)/shard_map/ppermute | solution.py:161
  16.8 2.9 %collective-permute-start.4 = (bf16[512,256]{1,0:T(8,128)(2,1)S(1)}, bf16[512,256]{1,0:T(8,128)(2,1)S(1)}, u32[]{:S(2)}, u32[]{:S(2)}) collective-permute-start(bf16[512,256]{1,0:T(8,128)(2,1)S(1)} %constant_dynamic-update-slice_fusion.2.refs_0_), channel_id=1, source_target_pairs={{0,32},{32,64},{64,96},{96,128},{128,160},{160,192},{192,224},{224... | collective-permute-start | bytes 786440 | tf_op jit(solution)/shard_map/ppermute | solution.py:165
  20.0 4.3 %collective-permute-done.4.refs_1_ = bf16[512,256]{1,0:T(8,128)(2,1)S(1)} collective-permute-done((bf16[512,256]{1,0:T(8,128)(2,1)S(1)}, bf16[512,256]{1,0:T(8,128)(2,1)S(1)}, u32[]{:S(2)}, u32[]{:S(2)}) %collective-permute-start.4) | collective-permute-done | bytes 262176 | tf_op jit(solution)/shard_map/ppermute | solution.py:165
  24.3 3.1 %collective-permute-start.5 = (bf16[512,256]{1,0:T(8,128)(2,1)S(1)}, bf16[512,256]{1,0:T(8,128)(2,1)S(1)}, u32[]{:S(2)}, u32[]{:S(2)}) collective-permute-start(bf16[512,256]{1,0:T(8,128)(2,1)S(1)} %collective-permute-done.4.refs_1_), channel_id=1, source_target_pairs={{0,32},{32,64},{64,96},{96,128},{128,160},{160,192},{192,224},{224... | collective-permute-start | bytes 786440 | tf_op jit(solution)/shard_map/ppermute | solution.py:165
  28.3 4.7 %collective-permute-done.5.refs_2_ = bf16[512,256]{1,0:T(8,128)(2,1)S(1)} collective-permute-done((bf16[512,256]{1,0:T(8,128)(2,1)S(1)}, bf16[512,256]{1,0:T(8,128)(2,1)S(1)}, u32[]{:S(2)}, u32[]{:S(2)}) %collective-permute-start.5) | collective-permute-done | bytes 262176 | tf_op jit(solution)/shard_map/ppermute | solution.py:165
  33.0 3.1 %collective-permute-start.6 = (bf16[512,256]{1,0:T(8,128)(2,1)S(1)}, bf16[512,256]{1,0:T(8,128)(2,1)}, u32[]{:S(2)}, u32[]{:S(2)}) collective-permute-start(bf16[512,256]{1,0:T(8,128)(2,1)S(1)} %collective-permute-done.5.refs_2_), channel_id=1, source_target_pairs={{0,32},{32,64},{64,96},{96,128},{128,160},{160,192},{192,224},{224... | collective-permute-start | bytes 786440 | tf_op jit(solution)/shard_map/ppermute | solution.py:165
  37.3 5.4 %all-to-all-start = ((bf16[32,8,1024]{2,1,0:T(8,128)(2,1)}), bf16[32,8,1024]{2,1,0:T(8,128)(2,1)S(1)}, u32[]{:S(2)}, u32[]{:S(2)}) async-start(bf16[32,8,1024]{2,1,0:T(8,128)(2,1)} %fusion), calls=%async_computation | async-start | bytes 1048576 | tf_op jit(solution)/shard_map/all_to_all | solution.py:200
  43.9 2.4 %collective-permute-start.7 = (bf16[512,256]{1,0:T(8,128)(2,1)}, bf16[512,256]{1,0:T(8,128)(2,1)}, u32[]{:S(2)}, u32[]{:S(2)}) collective-permute-start(bf16[512,256]{1,0:T(8,128)(2,1)} %collective-permute-done.6.refs_3_), channel_id=1, source_target_pairs={{0,32},{32,64},{64,96},{96,128},{128,160},{160,192},{192,224},{224... | collective-permute-start | bytes 786440 | tf_op jit(solution)/shard_map/ppermute | solution.py:165
  46.4 2.8 %collective-permute-start.1 = (bf16[256,1024]{1,0:T(8,128)(2,1)S(1)}, bf16[256,1024]{1,0:T(8,128)(2,1)S(1)}, u32[]{:S(2)}, u32[]{:S(2)}) collective-permute-start(bf16[256,1024]{1,0:T(8,128)(2,1)S(1)} %bitcast.34), channel_id=1, source_target_pairs={{0,0},{1,8},{8,1},{9,9},{2,2},{3,10},{10,3},{11,11},{4,4},{5,12},{... | collective-permute-start | bytes 1572872 | tf_op jit(solution)/shard_map/ppermute | solution.py:161
  50.1 12.9 %collective-permute-done.10.refs_5_ = bf16[512,256]{1,0:T(8,128)(2,1)} collective-permute-done((bf16[512,256]{1,0:T(8,128)(2,1)}, bf16[512,256]{1,0:T(8,128)(2,1)}, u32[]{:S(2)}, u32[]{:S(2)}) %collective-permute-start.10) | collective-permute-done | bytes 262176 | tf_op jit(solution)/shard_map/ppermute | solution.py:165
  66.5 41.2 %attend.1 = (bf16[256,1024]{1,0:T(8,128)(2,1)}, bf16[256,1024]{1,0:T(8,128)(2,1)}, bf16[512,256]{1,0:T(8,128)(2,1)S(1)}, bf16[512,256]{1,0:T(8,128)(2,1)S(1)}, b...) custom-call(s32[8]{0:T(128)S(1)} %get-tuple-element.46.lo_ref, ...), custom_call_target="tpu_custom_call" | custom-call | flops 12000000000 | bytes 12000000 | tf_op jit(solution)/shard_map/attend/pallas_call | solution.py:132
  109.9 9.2 %all-to-all-start.2 = ((bf16[32,8,1024]{2,1,0:T(8,128)(2,1)}), bf16[32,8,1024]{2,1,0:T(8,128)(2,1)S(1)}, u32[]{:S(2)}, u32[]{:S(2)}) async-start(bf16[32,8,1024]{2,1,0:T(8,128)(2,1)} %bitcast.10), calls=%async_computation.2 | async-start | bytes 1048576 | tf_op jit(solution)/shard_map/all_to_all | solution.py:228
  119.6 2.1 %collective-permute-start.19 = (bf16[256,1024]{1,0:T(8,128)(2,1)}, bf16[256,1024]{1,0:T(8,128)(2,1)S(1)}, u32[]{:S(2)}, u32[]{:S(2)}) collective-permute-start(bf16[256,1024]{1,0:T(8,128)(2,1)} %get-tuple-element.22), channel_id=1, source_target_pairs={{0,0},{1,8},{8,1},{9,9},{2,2},{3,10},{10,3},{11,11},{4,4},{5,12},{... | collective-permute-start | bytes 1572872 | tf_op jit(solution)/shard_map/ppermute | solution.py:161
  123.7 2.5 %collective-permute-start.27 = (bf16[512,256]{1,0:T(8,128)(2,1)S(1)}, bf16[512,256]{1,0:T(8,128)(2,1)S(1)}, u32[]{:S(2)}, u32[]{:S(2)}) collective-permute-start(bf16[512,256]{1,0:T(8,128)(2,1)S(1)} %add_convert_fusion.7), channel_id=1, source_target_pairs={{0,32},{32,64},{64,96},{96,128},{128,160},{160,192},{192,224},{224... | collective-permute-start | bytes 786440 | tf_op jit(solution)/shard_map/ppermute | solution.py:165
  127.0 12.4 %collective-permute-done.33 = bf16[512,256]{1,0:T(8,128)(2,1)S(1)} collective-permute-done((bf16[512,256]{1,0:T(8,128)(2,1)S(1)}, bf16[512,256]{1,0:T(8,128)(2,1)S(1)}, u32[]{:S(2)}, u32[]{:S(2)}) %collective-permute-start.33) | collective-permute-done | bytes 262176 | tf_op jit(solution)/shard_map/ppermute | solution.py:165
  143.2 2.7 %collective-permute-start.28 = (bf16[512,256]{1,0:T(8,128)(2,1)}, bf16[512,256]{1,0:T(8,128)(2,1)}, u32[]{:S(2)}, u32[]{:S(2)}) collective-permute-start(bf16[512,256]{1,0:T(8,128)(2,1)} %add_convert_fusion.6), channel_id=1, source_target_pairs={{0,32},{32,64},{64,96},{96,128},{128,160},{160,192},{192,224},{224... | collective-permute-start | bytes 786440 | tf_op jit(solution)/shard_map/ppermute | solution.py:165
  146.2 3.0 %collective-permute-start.20 = (bf16[256,1024]{1,0:T(8,128)(2,1)S(1)}, bf16[256,1024]{1,0:T(8,128)(2,1)S(1)}, u32[]{:S(2)}, u32[]{:S(2)}) collective-permute-start(bf16[256,1024]{1,0:T(8,128)(2,1)S(1)} %convolution_convert_fusion), channel_id=1, source_target_pairs={{0,0},{1,8},{8,1},{9,9},{2,2},{3,10},{10,3},{11,11},{4,4},{5,12},{... | collective-permute-start | bytes 1572872 | tf_op jit(solution)/shard_map/ppermute | solution.py:161
  154.7 2.7 %collective-permute-start.29 = (bf16[512,256]{1,0:T(8,128)(2,1)}, bf16[512,256]{1,0:T(8,128)(2,1)}, u32[]{:S(2)}, u32[]{:S(2)}) collective-permute-start(bf16[512,256]{1,0:T(8,128)(2,1)} %add_convert_fusion.5), channel_id=1, source_target_pairs={{0,32},{32,64},{64,96},{96,128},{128,160},{160,192},{192,224},{224... | collective-permute-start | bytes 786440 | tf_op jit(solution)/shard_map/ppermute | solution.py:165
  159.4 6.4 %all-to-all-start.3 = ((bf16[8,32,1024]{2,1,0:T(8,128)(2,1)}), bf16[8,32,1024]{2,1,0:T(8,128)(2,1)S(1)}, u32[]{:S(2)}, u32[]{:S(2)}) async-start(bf16[8,32,1024]{2,1,0:T(8,128)(2,1)} %bitcast.13), calls=%async_computation.3 | async-start | bytes 1048576 | tf_op jit(solution)/shard_map/all_to_all | solution.py:230
  168.1 2.3 %collective-permute-start.36 = (bf16[256,256]{1,0:T(8,128)(2,1)S(1)}, bf16[256,256]{1,0:T(8,128)(2,1)S(1)}, u32[]{:S(2)}, u32[]{:S(2)}) collective-permute-start(bf16[256,256]{1,0:T(8,128)(2,1)S(1)} %get-tuple-element.40), channel_id=1, source_target_pairs={{0,0},{1,8},{8,1},{9,9},{2,2},{3,10},{10,3},{11,11},{4,4},{5,12},{... | collective-permute-start | bytes 393224 | tf_op jit(solution)/shard_map/ppermute | solution.py:161
  170.5 2.9 %collective-permute-start.37 = (bf16[256,256]{1,0:T(8,128)(2,1)S(1)}, bf16[256,256]{1,0:T(8,128)(2,1)S(1)}, u32[]{:S(2)}, u32[]{:S(2)}) collective-permute-start(bf16[256,256]{1,0:T(8,128)(2,1)S(1)} %get-tuple-element.41), channel_id=1, source_target_pairs={{0,16},{1,24},{8,17},{9,25},{16,0},{17,8},{24,1},{25,9},{2,18},{3,... | collective-permute-start | bytes 393224 | tf_op jit(solution)/shard_map/ppermute | solution.py:174
  (143 shorter events, 32.3 us)
Async XLA Ops:
  1.6 15.2 %collective-permute-start.2 = (bf16[256,256]{1,0:T(8,128)(2,1)S(1)}, bf16[256,256]{1,0:T(8,128)(2,1)S(1)}, u32[]{:S(2)}, u32[]{:S(2)}) collective-permute-start(bf16[256,256]{1,0:T(8,128)(2,1)S(1)} %constant_dynamic-update-slice_fusion), channel_id=1, source_target_pairs={{0,0},{1,8},{8,1},{9,9},{2,2},{3,10},{10,3},{11,11},{4,4},{5,12},{... | collective-permute-start | bytes 393224 | tf_op jit(solution)/shard_map/ppermute | solution.py:161
  8.9 28.3 %all-to-all-start.1 = ((bf16[32,8,1024]{2,0,1:T(8,128)(2,1)}), bf16[32,8,1024]{2,0,1:T(8,128)(2,1)S(1)}, u32[]{:S(2)}, u32[]{:S(2)}) async-start(bf16[32,8,1024]{2,0,1:T(8,128)(2,1)} %bitcast.30), calls=%async_computation.1 | async-start | bytes 1048576 | tf_op jit(solution)/shard_map/all_to_all | solution.py:201
  13.6 22.5 %collective-permute-start = (bf16[256,1024]{1,0:T(8,128)(2,1)S(1)}, bf16[256,1024]{1,0:T(8,128)(2,1)S(1)}, u32[]{:S(2)}, u32[]{:S(2)}) collective-permute-start(bf16[256,1024]{1,0:T(8,128)(2,1)S(1)} %copy-done.6), channel_id=1, source_target_pairs={{0,0},{1,8},{8,1},{9,9},{2,2},{3,10},{10,3},{11,11},{4,4},{5,12},{... | collective-permute-start | bytes 1572872 | tf_op jit(solution)/shard_map/ppermute | solution.py:161
  27.7 15.9 %collective-permute-start.11 = (bf16[512,256]{1,0:T(8,128)(2,1)S(1)}, bf16[512,256]{1,0:T(8,128)(2,1)S(1)}, u32[]{:S(2)}, u32[]{:S(2)}) collective-permute-start(bf16[512,256]{1,0:T(8,128)(2,1)S(1)} %constant_dynamic-update-slice_fusion.2.refs_0_), channel_id=1, source_target_pairs={{0,1},{1,0},{2,3},{3,2},{4,5},{5,4},{6,7},{7,6},{8,9},{9,8},{10,11... | collective-permute-start | bytes 786440 | tf_op jit(solution)/shard_map/ppermute | solution.py:169
  27.9 18.5 %collective-permute-start.18 = (bf16[512,256]{1,0:T(8,128)(2,1)S(1)}, bf16[512,256]{1,0:T(8,128)(2,1)}, u32[]{:S(2)}, u32[]{:S(2)}) collective-permute-start(bf16[512,256]{1,0:T(8,128)(2,1)S(1)} %collective-permute-done.8.refs_7_), channel_id=1, source_target_pairs={{0,1},{1,0},{2,3},{3,2},{4,5},{5,4},{6,7},{7,6},{8,9},{9,8},{10,11... | collective-permute-start | bytes 786440 | tf_op jit(solution)/shard_map/ppermute | solution.py:169
  28.3 15.2 %collective-permute-start.9 = (bf16[512,256]{1,0:T(8,128)(2,1)S(1)}, bf16[512,256]{1,0:T(8,128)(2,1)}, u32[]{:S(2)}, u32[]{:S(2)}) collective-permute-start(bf16[512,256]{1,0:T(8,128)(2,1)S(1)} %collective-permute-done.8.refs_7_), channel_id=1, source_target_pairs={{0,224},{32,0},{64,32},{96,64},{128,96},{160,128},{192,160},{224,1... | collective-permute-start | bytes 786440 | tf_op jit(solution)/shard_map/ppermute | solution.py:165
  37.3 28.4 %all-to-all-start = ((bf16[32,8,1024]{2,1,0:T(8,128)(2,1)}), bf16[32,8,1024]{2,1,0:T(8,128)(2,1)S(1)}, u32[]{:S(2)}, u32[]{:S(2)}) async-start(bf16[32,8,1024]{2,1,0:T(8,128)(2,1)} %fusion), calls=%async_computation | async-start | bytes 1048576 | tf_op jit(solution)/shard_map/all_to_all | solution.py:200
  43.6 19.4 %collective-permute-start.10 = (bf16[512,256]{1,0:T(8,128)(2,1)}, bf16[512,256]{1,0:T(8,128)(2,1)}, u32[]{:S(2)}, u32[]{:S(2)}) collective-permute-start(bf16[512,256]{1,0:T(8,128)(2,1)} %collective-permute-done.9.refs_6_), channel_id=1, source_target_pairs={{0,224},{32,0},{64,32},{96,64},{128,96},{160,128},{192,160},{224,1... | collective-permute-start | bytes 786440 | tf_op jit(solution)/shard_map/ppermute | solution.py:165
  43.9 19.9 %collective-permute-start.7 = (bf16[512,256]{1,0:T(8,128)(2,1)}, bf16[512,256]{1,0:T(8,128)(2,1)}, u32[]{:S(2)}, u32[]{:S(2)}) collective-permute-start(bf16[512,256]{1,0:T(8,128)(2,1)} %collective-permute-done.6.refs_3_), channel_id=1, source_target_pairs={{0,32},{32,64},{64,96},{96,128},{128,160},{160,192},{192,224},{224... | collective-permute-start | bytes 786440 | tf_op jit(solution)/shard_map/ppermute | solution.py:165
  46.4 18.1 %collective-permute-start.1 = (bf16[256,1024]{1,0:T(8,128)(2,1)S(1)}, bf16[256,1024]{1,0:T(8,128)(2,1)S(1)}, u32[]{:S(2)}, u32[]{:S(2)}) collective-permute-start(bf16[256,1024]{1,0:T(8,128)(2,1)S(1)} %bitcast.34), channel_id=1, source_target_pairs={{0,0},{1,8},{8,1},{9,9},{2,2},{3,10},{10,3},{11,11},{4,4},{5,12},{... | collective-permute-start | bytes 1572872 | tf_op jit(solution)/shard_map/ppermute | solution.py:161
  49.5 14.9 %collective-permute-start.13 = (bf16[512,256]{1,0:T(8,128)(2,1)S(1)}, bf16[512,256]{1,0:T(8,128)(2,1)S(1)}, u32[]{:S(2)}, u32[]{:S(2)}) collective-permute-start(bf16[512,256]{1,0:T(8,128)(2,1)S(1)} %collective-permute-done.5.refs_2_), channel_id=1, source_target_pairs={{0,1},{1,0},{2,3},{3,2},{4,5},{5,4},{6,7},{7,6},{8,9},{9,8},{10,11... | collective-permute-start | bytes 786440 | tf_op jit(solution)/shard_map/ppermute | solution.py:169
  49.6 15.7 %collective-permute-start.14 = (bf16[512,256]{1,0:T(8,128)(2,1)}, bf16[512,256]{1,0:T(8,128)(2,1)S(1)}, u32[]{:S(2)}, u32[]{:S(2)}) collective-permute-start(bf16[512,256]{1,0:T(8,128)(2,1)} %collective-permute-done.6.refs_3_), channel_id=1, source_target_pairs={{0,1},{1,0},{2,3},{3,2},{4,5},{5,4},{6,7},{7,6},{8,9},{9,8},{10,11... | collective-permute-start | bytes 786440 | tf_op jit(solution)/shard_map/ppermute | solution.py:169
  108.1 13.6 %collective-permute-start.32 = (bf16[512,256]{1,0:T(8,128)(2,1)}, bf16[512,256]{1,0:T(8,128)(2,1)S(1)}, u32[]{:S(2)}, u32[]{:S(2)}) collective-permute-start(bf16[512,256]{1,0:T(8,128)(2,1)} %get-tuple-element.39), channel_id=1, source_target_pairs={{0,1},{1,0},{2,3},{3,2},{4,5},{5,4},{6,7},{7,6},{8,9},{9,8},{10,11... | collective-permute-start | bytes 786440 | tf_op jit(solution)/shard_map/ppermute | solution.py:169
  108.2 13.9 %collective-permute-start.24 = (bf16[512,256]{1,0:T(8,128)(2,1)}, bf16[512,256]{1,0:T(8,128)(2,1)S(1)}, u32[]{:S(2)}, u32[]{:S(2)}) collective-permute-start(bf16[512,256]{1,0:T(8,128)(2,1)} %get-tuple-element.31), channel_id=1, source_target_pairs={{0,1},{1,0},{2,3},{3,2},{4,5},{5,4},{6,7},{7,6},{8,9},{9,8},{10,11... | collective-permute-start | bytes 786440 | tf_op jit(solution)/shard_map/ppermute | solution.py:169
  109.9 35.9 %all-to-all-start.2 = ((bf16[32,8,1024]{2,1,0:T(8,128)(2,1)}), bf16[32,8,1024]{2,1,0:T(8,128)(2,1)S(1)}, u32[]{:S(2)}, u32[]{:S(2)}) async-start(bf16[32,8,1024]{2,1,0:T(8,128)(2,1)} %bitcast.10), calls=%async_computation.2 | async-start | bytes 1048576 | tf_op jit(solution)/shard_map/all_to_all | solution.py:228
  119.6 20.7 %collective-permute-start.19 = (bf16[256,1024]{1,0:T(8,128)(2,1)}, bf16[256,1024]{1,0:T(8,128)(2,1)S(1)}, u32[]{:S(2)}, u32[]{:S(2)}) collective-permute-start(bf16[256,1024]{1,0:T(8,128)(2,1)} %get-tuple-element.22), channel_id=1, source_target_pairs={{0,0},{1,8},{8,1},{9,9},{2,2},{3,10},{10,3},{11,11},{4,4},{5,12},{... | collective-permute-start | bytes 1572872 | tf_op jit(solution)/shard_map/ppermute | solution.py:161
  121.8 17.6 %collective-permute-start.33 = (bf16[512,256]{1,0:T(8,128)(2,1)S(1)}, bf16[512,256]{1,0:T(8,128)(2,1)S(1)}, u32[]{:S(2)}, u32[]{:S(2)}) collective-permute-start(bf16[512,256]{1,0:T(8,128)(2,1)S(1)} %add_convert_fusion.4), channel_id=1, source_target_pairs={{0,224},{32,0},{64,32},{96,64},{128,96},{160,128},{192,160},{224,1... | collective-permute-start | bytes 786440 | tf_op jit(solution)/shard_map/ppermute | solution.py:165
  122.7 19.6 %collective-permute-start.23 = (bf16[512,256]{1,0:T(8,128)(2,1)S(1)}, bf16[512,256]{1,0:T(8,128)(2,1)S(1)}, u32[]{:S(2)}, u32[]{:S(2)}) collective-permute-start(bf16[512,256]{1,0:T(8,128)(2,1)S(1)} %copy-done.15), channel_id=1, source_target_pairs={{0,1},{1,0},{2,3},{3,2},{4,5},{5,4},{6,7},{7,6},{8,9},{9,8},{10,11... | collective-permute-start | bytes 786440 | tf_op jit(solution)/shard_map/ppermute | solution.py:169
  123.7 18.6 %collective-permute-start.27 = (bf16[512,256]{1,0:T(8,128)(2,1)S(1)}, bf16[512,256]{1,0:T(8,128)(2,1)S(1)}, u32[]{:S(2)}, u32[]{:S(2)}) collective-permute-start(bf16[512,256]{1,0:T(8,128)(2,1)S(1)} %add_convert_fusion.7), channel_id=1, source_target_pairs={{0,32},{32,64},{64,96},{96,128},{128,160},{160,192},{192,224},{224... | collective-permute-start | bytes 786440 | tf_op jit(solution)/shard_map/ppermute | solution.py:165
  126.2 40.8 %collective-permute-start.21 = (bf16[512,256]{1,0:T(8,128)(2,1)}, bf16[512,256]{1,0:T(8,128)(2,1)S(1)}, u32[]{:S(2)}, u32[]{:S(2)}) collective-permute-start(bf16[512,256]{1,0:T(8,128)(2,1)} %get-tuple-element.25), channel_id=1, source_target_pairs={{0,1},{1,0},{2,3},{3,2},{4,5},{5,4},{6,7},{7,6},{8,9},{9,8},{10,11... | collective-permute-start | bytes 786440 | tf_op jit(solution)/shard_map/ppermute | solution.py:169
  139.4 13.5 %collective-permute-start.22 = (bf16[512,256]{1,0:T(8,128)(2,1)}, bf16[512,256]{1,0:T(8,128)(2,1)}, u32[]{:S(2)}, u32[]{:S(2)}) collective-permute-start(bf16[512,256]{1,0:T(8,128)(2,1)} %get-tuple-element.27), channel_id=1, source_target_pairs={{0,1},{1,0},{2,3},{3,2},{4,5},{5,4},{6,7},{7,6},{8,9},{9,8},{10,11... | collective-permute-start | bytes 786440 | tf_op jit(solution)/shard_map/ppermute | solution.py:169
  146.2 19.6 %collective-permute-start.20 = (bf16[256,1024]{1,0:T(8,128)(2,1)S(1)}, bf16[256,1024]{1,0:T(8,128)(2,1)S(1)}, u32[]{:S(2)}, u32[]{:S(2)}) collective-permute-start(bf16[256,1024]{1,0:T(8,128)(2,1)S(1)} %convolution_convert_fusion), channel_id=1, source_target_pairs={{0,0},{1,8},{8,1},{9,9},{2,2},{3,10},{10,3},{11,11},{4,4},{5,12},{... | collective-permute-start | bytes 1572872 | tf_op jit(solution)/shard_map/ppermute | solution.py:161
  152.9 14.1 %collective-permute-start.35 = (bf16[512,256]{1,0:T(8,128)(2,1)}, bf16[512,256]{1,0:T(8,128)(2,1)S(1)}, u32[]{:S(2)}, u32[]{:S(2)}) collective-permute-start(bf16[512,256]{1,0:T(8,128)(2,1)} %add_convert_fusion.2), channel_id=1, source_target_pairs={{0,224},{32,0},{64,32},{96,64},{128,96},{160,128},{192,160},{224,1... | collective-permute-start | bytes 786440 | tf_op jit(solution)/shard_map/ppermute | solution.py:165
  159.4 14.7 %all-to-all-start.3 = ((bf16[8,32,1024]{2,1,0:T(8,128)(2,1)}), bf16[8,32,1024]{2,1,0:T(8,128)(2,1)S(1)}, u32[]{:S(2)}, u32[]{:S(2)}) async-start(bf16[8,32,1024]{2,1,0:T(8,128)(2,1)} %bitcast.13), calls=%async_computation.3 | async-start | bytes 1048576 | tf_op jit(solution)/shard_map/all_to_all | solution.py:230
  (34 other events, 250.5 us)
